TPU v7x, 128 devices: a whole 4x4x4 slice. The times are simulated.
128 devices in a mesh: child: 8 (over z, core), grp: 16 (over y, x).
Axes of the slice: x: 4, y: 4, z: 4, core: 2. Of those that a mesh axis runs over, the one named last changes fastest.
Arguments:
- front_child: float32 [8, 4096, 4096], P('child', 'grp'), may hold values from -6 to 6
- left_factor: float32 [8, 4096, 1280], P('child', 'grp'), may hold values from -0.15625 to 0.15625
- right_factor: float32 [8, 1280, 4096], P('child', None, 'grp'), may hold values from -6 to 6
- child_map: int32 [8, 32], replicated, may hold values from 0 to 127, as said below
- parent_diag: float32 [16384], replicated, may hold values from 1 to 8
- lead_block: float32 [128, 128], replicated, may hold values from -4 to 304
- pivots: int32 [128], replicated, may hold values from 0 to 127, as said below
Outputs:
- front: float32 [8, 2048, 16, 1024], P('child', None, 'grp')
Inputs may be any that keep to these rules, and one draw needn't show every extreme that they name: `child_map`: row k names the parent tile of each of child k's tiles; one child's tiles are distinct; of one child's tiles at most 3 have one value modulo 16, and at most 6 one value modulo 8; both bounds are reached by every child. `pivots`: A permutation of the first 128 rows.
All inputs are finite; a program needn't handle non-finite values.
Results may differ from a plain program's by a relative error of at most 0.0001.
Values sent between devices are 32-bit elements; how exact they have to be, the bound alone decides.
A program may use at most 128 MiB of HBM per device.

v0:
```python
import jax
import jax.numpy as jnp
from jax import lax
from jax.sharding import PartitionSpec as P

NB = 128
CB = 4096
NP = 16384


full_precision = lax.Precision.HIGHEST


def from_root(shard, axis, root):
    mine = lax.axis_index(axis) == root
    return lax.psum(jnp.where(mine, shard, jnp.zeros_like(shard)), axis)


def factor_tile(square):
    order_n = square.shape[0]
    positions = jnp.arange(order_n)

    def eliminate(j, working):
        pivot_value = working[j, j]
        column = jnp.where(positions > j, working[:, j] / pivot_value, 0.0)
        row_part = jnp.where(positions > j, working[j, :], 0.0)
        working = working - column[:, None] * row_part[None, :]
        working = working.at[:, j].set(jnp.where(positions > j, column, working[:, j]))
        return working

    return lax.fori_loop(0, order_n, eliminate, square)


def lower_inverse(lower, unit):
    order_n = lower.shape[0]
    positions = jnp.arange(order_n)
    identity = jnp.eye(order_n, dtype=jnp.float32)

    def substitute(j, inverse):
        coeffs = jnp.where(positions < j, lower[j, :], 0.0)
        row_new = identity[j] - jnp.dot(
            coeffs, inverse, precision=full_precision, preferred_element_type=jnp.float32
        )
        if not unit:
            row_new = row_new / lower[j, j]
        return inverse.at[j].set(row_new)

    return lax.fori_loop(0, order_n, substitute, jnp.zeros((order_n, order_n), jnp.float32))


def slot_table(classes, groups, capacity):
    count_tiles = classes.shape[0]
    places = jnp.arange(count_tiles)
    same_class = classes[:, None] == classes[None, :]
    before = places[None, :] < places[:, None]
    ranked = jnp.sum((same_class & before).astype(jnp.int32), axis=1)
    matches = (classes[None, None, :] == jnp.arange(groups)[:, None, None]) & (
        ranked[None, None, :] == jnp.arange(capacity)[None, :, None]
    )
    picked = jnp.sum(jnp.where(matches, places[None, None, :], 0), axis=2)
    filled = jnp.any(matches, axis=2)
    return (picked, filled)


def body(front_child, left_factor, right_factor, child_map, parent_diag, lead_block, pivots):
    groups = lax.axis_size("grp")
    rowgroups = lax.axis_size("child")
    child_index = lax.axis_index("child")
    group_index = lax.axis_index("grp")
    tiles_child = CB // NB
    capacity_cols = tiles_child // groups + 1
    capacity_rows = capacity_cols * (groups // rowgroups)
    tile_rows = NP // NB // rowgroups
    tile_cols = NP // NB // groups
    local_front = front_child[0]
    local_left = left_factor[0]
    local_right = right_factor[0]
    slot_width = capacity_cols * NB
    cols_picked, cols_filled = jax.vmap(
        lambda tile_map: slot_table(tile_map % groups, groups, capacity_cols)
    )(child_map)
    rows_picked, rows_filled = jax.vmap(
        lambda tile_map: slot_table(tile_map % rowgroups, rowgroups, capacity_rows)
    )(child_map)
    col_pick = lax.dynamic_index_in_dim(cols_picked, child_index, 0, keepdims=False)
    col_fill = lax.dynamic_index_in_dim(cols_filled, child_index, 0, keepdims=False)
    contribution = local_front - jnp.dot(
        local_left,
        lax.all_gather(local_right, "grp", axis=1, tiled=True),
        precision=full_precision,
        preferred_element_type=jnp.float32,
    )
    tile_view = contribution.reshape(contribution.shape[0], tiles_child, NB)
    chosen = jnp.take(tile_view, col_pick.reshape(-1), axis=1) * col_fill.reshape(1, -1, 1).astype(
        jnp.float32
    )
    by_column = lax.all_to_all(
        chosen.reshape(contribution.shape[0], groups, slot_width),
        "grp",
        split_axis=1,
        concat_axis=0,
        tiled=True,
    )
    by_column = by_column.reshape(tiles_child, NB, slot_width)
    row_pick = lax.dynamic_index_in_dim(rows_picked, child_index, 0, keepdims=False)
    row_fill = lax.dynamic_index_in_dim(rows_filled, child_index, 0, keepdims=False)
    second = jnp.take(by_column, row_pick.reshape(-1), axis=0) * row_fill.reshape(-1, 1, 1).astype(
        jnp.float32
    )
    second = second.reshape(rowgroups, capacity_rows * NB, slot_width)
    arrived = lax.all_to_all(second, "child", split_axis=0, concat_axis=0, tiled=True)
    col_pick_all = lax.dynamic_index_in_dim(cols_picked, group_index, 1, keepdims=False)
    col_fill_all = lax.dynamic_index_in_dim(cols_filled, group_index, 1, keepdims=False)
    row_pick_all = lax.dynamic_index_in_dim(rows_picked, child_index, 1, keepdims=False)
    row_fill_all = lax.dynamic_index_in_dim(rows_filled, child_index, 1, keepdims=False)
    col_tiles = jnp.take_along_axis(child_map, col_pick_all, axis=1) // groups
    row_tiles = jnp.take_along_axis(child_map, row_pick_all, axis=1) // rowgroups
    row_hot = (
        (row_tiles[:, None, :] == jnp.arange(tile_rows)[None, :, None]) & row_fill_all[:, None, :]
    ).astype(jnp.float32)
    col_hot = (
        (col_tiles[:, None, :] == jnp.arange(tile_cols)[None, :, None]) & col_fill_all[:, None, :]
    ).astype(jnp.float32)
    blocks = arrived.reshape(rowgroups, capacity_rows, NB, capacity_cols, NB)
    placed = jnp.einsum("kar,krisj->kaisj", row_hot, blocks, precision=full_precision)
    parent_front = jnp.einsum("kaisj,kbs->aibj", placed, col_hot, precision=full_precision).reshape(
        tile_rows * NB, tile_cols * NB
    )
    row_global = (
        (jnp.arange(tile_rows)[:, None] * rowgroups + child_index) * NB + jnp.arange(NB)[None, :]
    ).reshape(-1)
    col_global = (
        (jnp.arange(tile_cols)[:, None] * groups + group_index) * NB + jnp.arange(NB)[None, :]
    ).reshape(-1)
    on_diag = row_global[:, None] == col_global[None, :]
    parent_front = parent_front + jnp.where(
        on_diag, jnp.take(parent_diag, row_global)[:, None], 0.0
    )
    is_first_row = child_index == 0
    is_first_col = group_index == 0
    is_owner = is_first_row & is_first_col
    parent_front = parent_front.at[:NB, :NB].add(jnp.where(is_owner, lead_block, 0.0))
    top_rows = jnp.take(parent_front[:NB, :], pivots, axis=0)
    lead_tile = jnp.where(is_owner, top_rows[:, :NB], jnp.eye(NB, dtype=jnp.float32))
    packed_own = factor_tile(lead_tile)
    packed_col = from_root(packed_own, ("child", "grp"), 0)
    upper_part = jnp.triu(packed_col)
    lower_part = jnp.tril(packed_col, -1) + jnp.eye(NB, dtype=jnp.float32)
    upper_inverse = lower_inverse(upper_part.T, False).T
    unit_inverse = lower_inverse(lower_part, True)
    left_raw = jnp.dot(
        parent_front[:, :NB],
        upper_inverse,
        precision=full_precision,
        preferred_element_type=jnp.float32,
    )
    right_raw = jnp.dot(
        unit_inverse, top_rows, precision=full_precision, preferred_element_type=jnp.float32
    )
    row_lead = row_global < NB
    col_lead = col_global < NB
    left_send = jnp.where(row_lead[:, None], 0.0, left_raw)
    right_send = jnp.where(col_lead[None, :], 0.0, right_raw)
    left_all = from_root(left_send, "grp", 0)
    right_all = from_root(right_send, "child", 0)
    updated = parent_front - jnp.dot(
        left_all, right_all, precision=full_precision, preferred_element_type=jnp.float32
    )
    left_out = jnp.where(row_lead[:, None], updated[:, :NB], left_raw)
    updated = updated.at[:, :NB].set(jnp.where(is_first_col, left_out, updated[:, :NB]))
    top_out = right_raw.at[:, :NB].set(jnp.where(is_first_col, packed_col, right_raw[:, :NB]))
    updated = updated.at[:NB, :].set(jnp.where(is_first_row, top_out, updated[:NB, :]))
    return updated.reshape(1, tile_rows * NB, 1, tile_cols * NB)


def solution(mesh):
    in_specs = (
        P("child", "grp", None),
        P("child", "grp", None),
        P("child", None, "grp"),
        P(),
        P(),
        P(),
        P(),
    )
    out_specs = P("child", None, "grp", None)
    return jax.shard_map(body, mesh=mesh, in_specs=in_specs, out_specs=out_specs, check_vma=False)
```

profile of v0, /device:TPU:1, one launch (start us, length us, event | category | flops | bytes accessed | tf_op | source)
XLA Modules:
  0.0 1813.4 jit_solution(16405330948753583068)
XLA Ops:
  10.1 144.0 %all-gather.3.cloned.1.call-done = f32[1,1280,4096]{2,1,0:T(8,128)} async-done(((f32[1,1280,256]{2,1,0:T(8,128)}), f32[1,1280,4096]{2,1,0:T(8,128)}) %all-gather.3.cloned.1.call-update) | async-done | bytes 20971536 | tf_op jit(solution)/shard_map/all_gather | solution.py:89
  154.1 21.3 %fusion.34 = f32[32,32,8,128]{3,2,1,0:T(8,128)S(1)} fusion(f32[1,1280,4096]{2,1,0:T(8,128)} %all-gather.3.cloned.1.call-done, f32[1,256,4096]{2,1,0:T(8,128)} %param.27, f32[1,256,1280]{2,1,0:T(8,128)S(1)} %copy-done), kind=kOutput, calls=%fused_computation.62 | convolution fusion | flops 16107175936 | bytes 30670848 | tf_op jit(solution)/shard_map/dot_general | solution.py:87
  175.4 2.4 copy.131
  177.9 5.8 gather_fusion
  183.7 6.6 copy.104
  190.3 7.6 fusion.30
  197.9 4.7 all-to-all-start
  204.9 88.8 %all-to-all-done = f32[256,16,384]{0,2,1:T(8,128)} async-done(((f32[256,16,384]{0,2,1:T(8,128)}), f32[256,16,384]{0,2,1:T(8,128)}, u32[]{:S(2)}, u32[]{:S(2)}) %all-to-all-start) | async-done | bytes 6291488 | tf_op jit(solution)/shard_map/all_to_all | solution.py:97
  293.7 6.6 copy.106
  300.2 7.6 gather_fusion.1
  307.8 9.6 copy.108
  317.4 8.4 select_multiply_fusion
  325.8 7.8 all-to-all-start.1
  336.8 11.8 gather_fusion.2
  349.6 89.2 %all-to-all-done.1 = f32[8,768,384]{1,2,0:T(8,128)} async-done(((f32[8,768,384]{1,2,0:T(8,128)}), f32[8,768,384]{1,2,0:T(8,128)}, u32[]{:S(2)}, u32[]{:S(2)}) %all-to-all-start.1) | async-done | bytes 9437216 | tf_op jit(solution)/shard_map/all_to_all | solution.py:111
  438.8 11.8 reshape.660
  450.5 12.7 copy.111
  463.2 18.1 %fusion.53 = f32[8,16,128,3,128]{4,1,3,2,0:T(8,128)} fusion(f32[8,6,128,3,128]{4,1,3,2,0:T(8,128)} %copy.111, s32[8,6]{1,0:T(8,128)S(1)} %fusion.49, pred[8,6]{1,0:T(8,128)(4,1)S(1)} %dynamic-slice_reduce_fusion), kind=kOutput, calls=%fused_computation.110 | convolution fusion | flops 452986368 | bytes 34603248 | tf_op jit(solution)/shard_map/kar,krisj->kaisj/dot_general | solution.py:125
  481.4 28.4 %fusion.26 = f32[8,16,128,128,1]{3,0,4,2,1:T(8,128)S(1)} fusion(f32[8,16,128,3,128]{4,1,3,2,0:T(8,128)} %fusion.53, s32[8,3]{0,1:T(4,128)S(1)} %bitcast.248, pred[8,3]{0,1:T(4,128)(4,1)S(1)} %bitcast.249), kind=kOutput, calls=%fused_computation.51 | convolution fusion | flops 603980160 | bytes 33554552 | tf_op jit(solution)/shard_map/kaisj,kbs->aibj/dot_general | solution.py:126
  509.8 1.6 bitcast_add_fusion
  511.5 3.4 copy-done.4
  516.0 462.2 %while.49 = (s32[]{:T(128)}, f32[128,128]{0,1:T(8,128)S(1)}, s32[]{:T(128)}, s32[1]{0:T(128)}, s32[]{:T(128)}) while((s32[]{:T(128)}, f32[128,128]{0,1:T(8,128)S(1)}, s32[]{:T(128)}, s32[1]{0:T(128)}, s32[]{:T(128)}) %tuple.140), condition=%wide.region_8.9_spmd.clone, body=%wide.region_6.8_spmd.clone.sunk | while | flops 34061 | bytes 403542 | solution.py:31
  979.0 135.4 %all-reduce.4.cloned.1.call-done = f32[128,128]{1,0:T(8,128)} async-done(((f32[128,128]{1,0:T(8,128)}), f32[128,128]{1,0:T(8,128)}) %all-reduce.4.cloned.1.call-update) | async-done | bytes 65552 | tf_op jit(solution)/shard_map/psum | solution.py:16
  1115.4 215.2 %while.51 = (s32[]{:T(128)}, f32[128,128]{1,0:T(8,128)S(1)}, f32[128,128]{1,0:T(8,128)S(1)}, f32[128,128]{1,0:T(8,128)S(1)}, s32[]{:T(128)}, /*index=5*/s32[2]{0:T(128)S(1)}, s32[1]{0:T(128)}, s32[]{:T(128)}) while((s32[]{:T(128)}, f32[128,128]{1,0:T(8,128)S(1)}, f32[128,128]{1,0:T(8,128)S(1)}, f32[128,128]{1,0:T(8,128)S(1)}, ...), condition=%wide.region_16.17_spmd.clone, body=%wide.region_14.16_spmd.clone.sunk | while | flops 197131 | bytes 70762 | solution.py:48
  1330.6 1.4 select_select_fusion.2
  1332.2 360.4 %while.50 = (s32[]{:T(128)}, f32[128,128]{1,0:T(8,128)S(1)}, f32[128,128]{1,0:T(8,128)S(1)}, f32[128,128]{1,0:T(8,128)S(1)}, s32[]{:T(128)}, /*index=5*/s32[2]{0:T(128)S(1)}, s32[1]{0:T(128)}, s32[]{:T(128)}) while((s32[]{:T(128)}, f32[128,128]{1,0:T(8,128)S(1)}, f32[128,128]{1,0:T(8,128)S(1)}, f32[128,128]{1,0:T(8,128)S(1)}, ...), condition=%wide.region_12.13_spmd.clone, body=%wide.region_10.12_spmd.clone.sunk | while | flops 197259 | bytes 71286 | solution.py:48
  1333.5 1.4 fusion.94
  1339.2 1.4 fusion.94
  1344.8 1.4 fusion.94
  1347.6 1.4 fusion.94
  1353.3 1.4 fusion.94
  1356.1 1.4 fusion.94
  1361.7 1.4 fusion.94
  1367.3 1.4 fusion.94
  1387.0 1.4 fusion.94
  1392.7 1.4 fusion.94
  1398.3 1.4 fusion.94
  1403.9 1.4 fusion.94
  1409.6 1.4 fusion.94
  1415.2 1.4 fusion.94
  1420.8 1.4 fusion.94
  1440.5 1.4 fusion.94
  1446.2 1.4 fusion.94
  1451.8 1.4 fusion.94
  1457.4 1.4 fusion.94
  1463.1 1.4 fusion.94
  1468.7 1.4 fusion.94
  1474.3 1.4 fusion.94
  1494.0 1.4 fusion.94
  1499.7 1.4 fusion.94
  1505.3 1.4 fusion.94
  1510.9 1.4 fusion.94
  1516.6 1.4 fusion.94
  1522.2 1.4 fusion.94
  1527.8 1.4 fusion.94
  1547.5 1.4 fusion.94
  1553.2 1.4 fusion.94
  1558.8 1.4 fusion.94
  1692.6 3.3 select_select_fusion.1
  1696.5 1.4 fusion.45
  1697.9 80.3 %all-reduce.6.cloned.1.call-done = f32[2048,128]{1,0:T(8,128)} async-done(((f32[2048,128]{1,0:T(8,128)}), f32[2048,128]{1,0:T(8,128)}) %all-reduce.6.cloned.1.call-update) | async-done | bytes 1048592 | tf_op jit(solution)/shard_map/psum | solution.py:16
  1778.2 9.7 convolution_subtract_fusion
  1789.0 1.7 copy.163
  1790.7 16.1 copy.116
  (2122 shorter events, 994.5 us)
Async XLA Ops:
  6.5 147.6 %copy-start = (f32[1,256,1280]{2,1,0:T(8,128)S(1)}, f32[1,256,1280]{2,1,0:T(8,128)}, u32[]{:S(2)}) copy-start(f32[1,256,1280]{2,1,0:T(8,128)} %param.28) | copy-start | bytes 3932164
  6.5 147.6 %all-gather.3.cloned.1.call-start = ((), (), s32[]{:S(2)}) async-start(), calls=%async_computation.5 | async-start | bytes 22282240 | tf_op jit(solution)/shard_map/all_gather | solution.py:89
  197.9 95.8 %all-to-all-start = ((f32[256,16,384]{0,2,1:T(8,128)}), f32[256,16,384]{0,2,1:T(8,128)}, u32[]{:S(2)}, u32[]{:S(2)}) async-start(f32[256,16,384]{0,2,1:T(8,128)} %fusion.30), calls=%async_computation | async-start | bytes 12582912 | tf_op jit(solution)/shard_map/all_to_all | solution.py:97
  325.8 8.2 copy-start.2
  325.8 112.9 %all-to-all-start.1 = ((f32[8,768,384]{1,2,0:T(8,128)}), f32[8,768,384]{1,2,0:T(8,128)}, u32[]{:S(2)}, u32[]{:S(2)}) async-start(f32[8,768,384]{1,2,0:T(8,128)} %select_multiply_fusion), calls=%async_computation.1 | async-start | bytes 18874368 | tf_op jit(solution)/shard_map/all_to_all | solution.py:111
  333.6 3.2 copy-start.3
  333.6 780.8 %all-reduce.4.cloned.1.call-start = ((), (), s32[]{:S(2)}) async-start(), calls=%async_computation.2 | async-start | bytes 131072 | tf_op jit(solution)/shard_map/psum | solution.py:16
  334.1 14.9 copy-start.7
  509.8 1.6 copy-start.5
  511.4 603.9 %copy-start.6 = (s32[2]{0:T(128)S(1)}, s32[2]{0:T(128)}, u32[]{:S(2)}) copy-start(s32[2]{0:T(128)} %constant.473.clone.2) | copy-start | bytes 28
  511.5 3.4 copy-start.4
  978.9 719.0 %all-reduce.8.cloned.1.call-start = ((), (), s32[]{:S(2)}) async-start(), calls=%async_computation.4 | async-start | bytes 1048576 | tf_op jit(solution)/shard_map/psum | solution.py:16
  1332.0 446.2 %all-reduce.6.cloned.1.call-start = ((), (), s32[]{:S(2)}) async-start(), calls=%async_computation.3 | async-start | bytes 2097152 | tf_op jit(solution)/shard_map/psum | solution.py:16
  1790.7 16.2 copy-start.1
Sparse Core Ops, SparseCore 0:
  9.5 144.5 all-gather.2
  979.1 135.3 all-reduce.3
  1332.1 55.9 all-reduce.7
  1696.0 82.1 all-reduce.5
where the time goes:
time: 1820 us; the launch traced here: 1810 us
  other arithmetic  581 us (32%)
  waiting for transfers between devices  538 us (30%)
  matrix products  369 us (20%)
  local copies, waits for them, and re-layouts  285 us (16%)
    another operation x513, other arithmetic  453 us
    dot_general x256, matrix products, substitute(): jnp.dot(coeffs, inverse, precision=full_precision, preferred_element_type...  287 us
    psum x3, waiting for transfers between devices, from_root(): return lax.psum(jnp.where(mine, shard, jnp.zeros_like(shard)), axis)  216 us
    all_gather x1, waiting for transfers between devices, body(): lax.all_gather(local_right, 'grp', axis=1, tiled=True)  144 us
    mul x256, other arithmetic, eliminate(): working = working - column[:, None] * row_part[None, :]  90.9 us
    all_to_all x1, waiting for transfers between devices, body(): lax.all_to_all(second, 'child', split_axis=0, concat_axis=0, tiled=True)  89.2 us
    all_to_all x1, waiting for transfers between devices, body(): lax.all_to_all(chosen.reshape(contribution.shape[0], groups, slot_width),...  88.8 us
    dynamic_slice x128, local copies, waits for them, and re-layouts, eliminate(): pivot_value = working[j, j]  85.5 us
  transfers between devices with their start and end apart: 6, of which 5 were waited for; matrix products, arithmetic and copies ran while one was open for 21% of the time, Pallas kernels for 0%

commit v1 on v0

--- a/solution.py
+++ b/solution.py
@@ -1,6 +1,7 @@
 import jax
 import jax.numpy as jnp
 from jax import lax
+from jax.experimental import pallas as pl
 from jax.sharding import PartitionSpec as P
 
 NB = 128
@@ -16,36 +17,39 @@
     return lax.psum(jnp.where(mine, shard, jnp.zeros_like(shard)), axis)
 
 
-def factor_tile(square):
-    order_n = square.shape[0]
-    positions = jnp.arange(order_n)
+def factor_kernel(tile_ref, packed_ref, lower_ref, upper_ref):
+    rows = lax.broadcasted_iota(jnp.int32, (NB, NB), 0)
+    cols = lax.broadcasted_iota(jnp.int32, (NB, NB), 1)
+    lane = lax.broadcasted_iota(jnp.int32, (1, NB), 1)
+    eye = jnp.where(rows == cols, 1.0, 0.0)
+    packed_ref[...] = tile_ref[...]
+    lower_ref[...] = eye
+    upper_ref[...] = eye
 
-    def eliminate(j, working):
-        pivot_value = working[j, j]
-        column = jnp.where(positions > j, working[:, j] / pivot_value, 0.0)
-        row_part = jnp.where(positions > j, working[j, :], 0.0)
-        working = working - column[:, None] * row_part[None, :]
-        working = working.at[:, j].set(jnp.where(positions > j, column, working[:, j]))
-        return working
+    def eliminate(j, carry):
+        working = packed_ref[...]
+        upper = upper_ref[...]
+        row_part = packed_ref[pl.ds(j, 1), :]
+        row_lower = lower_ref[pl.ds(j, 1), :]
+        column = jnp.sum(jnp.where(cols == j, working, 0.0), axis=1, keepdims=True)
+        column_upper = jnp.sum(jnp.where(cols == j, upper, 0.0), axis=1, keepdims=True)
+        pivot_value = jnp.sum(jnp.where(lane == j, row_part, 0.0), axis=1, keepdims=True)
+        multiplier = jnp.where(rows[:, :1] > j, column / pivot_value, 0.0)
+        right = jnp.where(lane > j, row_part, 0.0)
+        packed_ref[...] = jnp.where(
+            (cols == j) & (rows > j), multiplier, working - multiplier * right
+        )
+        lower_ref[...] = lower_ref[...] - multiplier * row_lower
+        scaled = column_upper / pivot_value
+        upper_ref[...] = jnp.where(cols == j, scaled, upper - scaled * right)
+        return carry
 
-    return lax.fori_loop(0, order_n, eliminate, square)
+    lax.fori_loop(0, NB, eliminate, 0)
 
 
-def lower_inverse(lower, unit):
-    order_n = lower.shape[0]
-    positions = jnp.arange(order_n)
-    identity = jnp.eye(order_n, dtype=jnp.float32)
-
-    def substitute(j, inverse):
-        coeffs = jnp.where(positions < j, lower[j, :], 0.0)
-        row_new = identity[j] - jnp.dot(
-            coeffs, inverse, precision=full_precision, preferred_element_type=jnp.float32
-        )
-        if not unit:
-            row_new = row_new / lower[j, j]
-        return inverse.at[j].set(row_new)
-
-    return lax.fori_loop(0, order_n, substitute, jnp.zeros((order_n, order_n), jnp.float32))
+def factor_tile(square):
+    tile = jax.ShapeDtypeStruct((NB, NB), jnp.float32)
+    return pl.pallas_call(factor_kernel, out_shape=(tile, tile, tile))(square)
 
 
 def slot_table(classes, groups, capacity):
@@ -141,13 +145,8 @@
     is_owner = is_first_row & is_first_col
     parent_front = parent_front.at[:NB, :NB].add(jnp.where(is_owner, lead_block, 0.0))
     top_rows = jnp.take(parent_front[:NB, :], pivots, axis=0)
-    lead_tile = jnp.where(is_owner, top_rows[:, :NB], jnp.eye(NB, dtype=jnp.float32))
-    packed_own = factor_tile(lead_tile)
-    packed_col = from_root(packed_own, ("child", "grp"), 0)
-    upper_part = jnp.triu(packed_col)
-    lower_part = jnp.tril(packed_col, -1) + jnp.eye(NB, dtype=jnp.float32)
-    upper_inverse = lower_inverse(upper_part.T, False).T
-    unit_inverse = lower_inverse(lower_part, True)
+    lead_tile = from_root(top_rows[:, :NB], ("child", "grp"), 0)
+    packed_col, unit_inverse, upper_inverse = factor_tile(lead_tile)
     left_raw = jnp.dot(
         parent_front[:, :NB],
         upper_inverse,

time: 1820 us -> 853 us (0.47)
  other arithmetic: 581 us -> 26.4 us
  matrix products: 369 us -> 83 us
  local copies, waits for them, and re-layouts: 285 us -> 101 us
  waiting for transfers between devices: 538 us -> 598 us
    another operation x513 -> x1, other arithmetic: 453 us -> 0.61 us
    dot_general x256 -> x0, matrix products: 287 us -> none  [substitute(): jnp.dot(coeffs, inverse, precision=full_precision, preferred_element_type...]
    dynamic_slice x256 -> x0, local copies, waits for them, and re-layouts: 159 us -> none  [the longest x128 85.5 us: eliminate(): pivot_value = working[j, j]]
    mul x256 -> x0, other arithmetic: 90.9 us -> none  [eliminate(): working = working - column[:, None] * row_part[None, :]]
    psum x3, waiting for transfers between devices: 216 us -> 276 us  [from_root(): return lax.psum(jnp.where(mine, shard, jnp.zeros_like(shard)), axis)]
  transfers between devices with their start and end apart: 6 -> 6, of which waited for: 5 -> 6; matrix products, arithmetic and copies ran while one was open for 21% -> 3% of each run, Pallas kernels for 0% -> 0%
where the time goes in v1:
time: 853 us; the launch traced here: 851 us
  waiting for transfers between devices  598 us (70%)
  local copies, waits for them, and re-layouts  101 us (12%)
  matrix products  83 us (10%)
  other arithmetic  26.4 us (3%)
  Pallas kernels  16.2 us (2%)
  between operations  13.5 us (2%)
  starting transfers between devices  12.6 us (1%)
    psum x3, waiting for transfers between devices, from_root(): return lax.psum(jnp.where(mine, shard, jnp.zeros_like(shard)), axis)  276 us
    all_gather x1, waiting for transfers between devices, body(): lax.all_gather(local_right, 'grp', axis=1, tiled=True)  144 us
    all_to_all x1, waiting for transfers between devices, body(): lax.all_to_all(second, 'child', split_axis=0, concat_axis=0, tiled=True)  89.3 us
    all_to_all x1, waiting for transfers between devices, body(): lax.all_to_all(chosen.reshape(contribution.shape[0], groups, slot_width),...  88.8 us
    dot_general x1, matrix products, body(): jnp.einsum('kaisj,kbs->aibj', placed, col_hot, precision=full_precision)  28.4 us
    reshape x2, local copies, waits for them, and re-layouts, body(): blocks = arrived.reshape(rowgroups, capacity_rows, NB, capacity_cols, NB)  24.5 us
    dot_general x1, matrix products, body(): jnp.dot(local_left, lax.all_gather(local_right, 'grp', axis=1, tiled=True...  21.3 us
    dot_general x1, matrix products, body(): jnp.einsum('kar,krisj->kaisj', row_hot, blocks, precision=full_precision)  18.1 us
  transfers between devices with their start and end apart: 6, of which 6 were waited for; matrix products, arithmetic and copies ran while one was open for 3% of the time, Pallas kernels for 0%

profile of v1, /device:TPU:1, one launch (start us, length us, event | category | flops | bytes accessed | tf_op | source)
XLA Modules:
  0.0 851.2 jit_solution(6194513447847818665)
XLA Ops:
  6.5 0.7 all-gather.3.cloned.1.call-update
  7.3 0.7 add_select_fusion.3
  8.0 0.5 convert_reduce_fusion
  8.5 0.5 fusion.17
  9.0 0.1 copy.85
  9.1 0.1 reshape.483
  9.2 0.1 copy.84
  9.3 0.1 broadcast_in_dim.165
  9.4 0.5 and_reduce_fusion.1
  9.9 0.1 copy.88
  10.1 144.0 %all-gather.3.cloned.1.call-done = f32[1,1280,4096]{2,1,0:T(8,128)} async-done(((f32[1,1280,256]{2,1,0:T(8,128)}), f32[1,1280,4096]{2,1,0:T(8,128)}) %all-gather.3.cloned.1.call-update) | async-done | bytes 20971536 | tf_op jit(solution)/shard_map/all_gather | solution.py:93
  154.1 21.3 %fusion.8 = f32[32,32,8,128]{3,2,1,0:T(8,128)S(1)} fusion(f32[1,1280,4096]{2,1,0:T(8,128)} %all-gather.3.cloned.1.call-done, f32[1,256,4096]{2,1,0:T(8,128)} %param.15, f32[1,256,1280]{2,1,0:T(8,128)S(1)} %copy-done), kind=kOutput, calls=%fused_computation.17 | convolution fusion | flops 16107175936 | bytes 30670848 | tf_op jit(solution)/shard_map/dot_general | solution.py:91
  175.4 2.4 copy.111
  177.9 5.8 gather_fusion
  183.7 6.6 copy.87
  190.3 7.6 fusion.4
  197.9 4.7 all-to-all-start
  202.7 0.9 fusion.18
  203.6 0.1 copy.82
  203.6 0.1 reshape.485
  203.7 0.1 copy.83
  203.8 0.9 and_reduce_fusion
  204.9 88.8 %all-to-all-done = f32[256,16,384]{0,2,1:T(8,128)} async-done(((f32[256,16,384]{0,2,1:T(8,128)}), f32[256,16,384]{0,2,1:T(8,128)}, u32[]{:S(2)}, u32[]{:S(2)}) %all-to-all-start) | async-done | bytes 6291488 | tf_op jit(solution)/shard_map/all_to_all | solution.py:101
  293.7 6.6 copy.89
  300.2 7.6 gather_fusion.1
  307.8 9.6 %copy.91 = f32[8,768,384]{1,2,0:T(8,128)} copy(f32[8,768,384]{2,1,0:T(8,128)} %bitcast.113) | data formatting | bytes 18874368 | tf_op jit(solution)/shard_map/jit(_take)/gather | solution.py:111
  317.4 8.4 select_multiply_fusion
  325.8 7.8 all-to-all-start.1
  333.7 0.1 copy.79
  333.9 0.1 copy.80
  334.0 0.1 reshape.530
  334.1 0.9 gather_fusion.5
  334.9 0.1 gather.55
  335.1 0.1 copy.74
  335.4 0.7 gather_fusion.4
  336.2 0.1 gather.54
  336.3 0.1 add_select_fusion.1
  336.4 0.1 copy.77
  336.6 0.1 copy.78
  336.8 11.8 %gather_fusion.2 = f32[2048]{0:T(1024)S(1)} fusion(f32[16384]{0:T(1024)S(1)} %copy-done.3, s32[2048]{0:T(1024)S(1)} %broadcast_clamp_fusion), kind=kCustom, calls=%fused_computation.2 | custom fusion | bytes 24576 | tf_op jit(solution)/shard_map/jit(_take)/gather | solution.py:141
  348.6 0.3 dynamic-slice_reduce_fusion
  348.9 0.3 fusion.22
  349.5 89.3 %all-to-all-done.1 = f32[8,768,384]{1,2,0:T(8,128)} async-done(((f32[8,768,384]{1,2,0:T(8,128)}), f32[8,768,384]{1,2,0:T(8,128)}, u32[]{:S(2)}, u32[]{:S(2)}) %all-to-all-start.1) | async-done | bytes 9437216 | tf_op jit(solution)/shard_map/all_to_all | solution.py:115
  438.8 11.8 %reshape.486 = f32[8,6,128,3,128]{2,1,4,3,0:T(8,128)} reshape(f32[8,768,384]{1,2,0:T(8,128)} %all-to-all-done.1) | data formatting | bytes 18874368 | tf_op jit(solution)/shard_map/reshape | solution.py:128
  450.5 12.7 %copy.94 = f32[8,6,128,3,128]{4,1,3,2,0:T(8,128)} copy(f32[8,6,128,3,128]{2,1,4,3,0:T(8,128)} %reshape.486) | data formatting | bytes 18874368 | tf_op jit(solution)/shard_map/reshape | solution.py:128
  463.2 18.1 %fusion.26 = f32[8,16,128,3,128]{4,1,3,2,0:T(8,128)} fusion(f32[8,6,128,3,128]{4,1,3,2,0:T(8,128)} %copy.94, s32[8,6]{1,0:T(8,128)S(1)} %fusion.22, pred[8,6]{1,0:T(8,128)(4,1)S(1)} %dynamic-slice_reduce_fusion), kind=kOutput, calls=%fused_computation.59 | convolution fusion | flops 452986368 | bytes 34603248 | tf_op jit(solution)/shard_map/kar,krisj->kaisj/dot_general | solution.py:129
  481.4 28.4 %fusion = f32[8,16,128,128,1]{3,0,4,2,1:T(8,128)S(1)} fusion(f32[8,16,128,3,128]{4,1,3,2,0:T(8,128)} %fusion.26, s32[8,3]{0,1:T(4,128)S(1)} %bitcast.124, pred[8,3]{0,1:T(4,128)(4,1)S(1)} %bitcast.125), kind=kOutput, calls=%fused_computation.6 | convolution fusion | flops 603980160 | bytes 33554552 | tf_op jit(solution)/shard_map/kaisj,kbs->aibj/dot_general | solution.py:130
  509.8 1.6 bitcast_add_fusion
  511.5 3.4 copy-done.4
  514.9 0.8 gather_fusion.3
  515.7 0.1 broadcast_select_fusion
  515.8 0.6 slice_select_fusion.1
  516.6 135.4 %all-reduce.4.cloned.1.call-done.tile_ref = f32[128,128]{1,0:T(8,128)} async-done(((f32[128,128]{1,0:T(8,128)}), f32[128,128]{1,0:T(8,128)}) %all-reduce.4.cloned.1.call-update) | async-done | bytes 65552 | tf_op jit(solution)/shard_map/psum | solution.py:17
  652.0 16.2 %shard_map.73 = (f32[128,128]{1,0:T(8,128)}, f32[128,128]{1,0:T(8,128)}, f32[128,128]{1,0:T(8,128)}) custom-call(f32[128,128]{1,0:T(8,128)} %all-reduce.4.cloned.1.call-done.tile_ref), custom_call_target="tpu_custom_call" | custom-call | tf_op jit(solution)/shard_map/pallas_call | solution.py:52
  668.2 2.2 select_select_fusion.2
  670.5 3.2 select_select_fusion.1
  673.8 0.6 compare_reduce_fusion
  674.4 1.4 fusion.19
  675.8 50.6 %all-reduce.8.cloned.1.call-done = f32[128,1024]{1,0:T(8,128)} async-done(((f32[128,1024]{1,0:T(8,128)}), f32[128,1024]{1,0:T(8,128)}) %all-reduce.8.cloned.1.call-update) | async-done | bytes 524304 | tf_op jit(solution)/shard_map/psum | solution.py:17
  726.4 89.6 %all-reduce.6.cloned.1.call-done = f32[2048,128]{1,0:T(8,128)} async-done(((f32[2048,128]{1,0:T(8,128)}), f32[2048,128]{1,0:T(8,128)}) %all-reduce.6.cloned.1.call-update) | async-done | bytes 1048592 | tf_op jit(solution)/shard_map/psum | solution.py:17
  816.0 9.7 %convolution_subtract_fusion = f32[2048,1024]{1,0:T(8,128)S(1)} fusion(f32[2048,1024]{1,0:T(8,128)} %copy-done.4, f32[2048,128]{1,0:T(8,128)} %all-reduce.6.cloned.1.call-done, f32[128,1024]{1,0:T(8,128)} %all-reduce.8.cloned.1.call-done), kind=kOutput, calls=%fused_computation.15 | convolution fusion | flops 3223322624 | bytes 18350080 | tf_op jit(solution)/shard_map/dot_general | solution.py:165
  825.7 1.1 fusion.12
  826.8 1.7 copy.120
  828.5 16.1 %copy.96 = f32[1,2048,1,1024]{3,2,1,0:T(1,128)} copy(f32[1,2048,1,1024]{3,1,2,0:T(8,128)S(1)} %fusion.16) | data formatting | bytes 16777216 | tf_op jit(solution)/shard_map/scatter | solution.py:171
  (61 shorter events, 1.5 us)
Async XLA Ops:
  6.5 147.6 %copy-start = (f32[1,256,1280]{2,1,0:T(8,128)S(1)}, f32[1,256,1280]{2,1,0:T(8,128)}, u32[]{:S(2)}) copy-start(f32[1,256,1280]{2,1,0:T(8,128)} %param.16) | copy-start | bytes 3932164
  6.5 147.6 %all-gather.3.cloned.1.call-start = ((), (), s32[]{:S(2)}) async-start(), calls=%async_computation.5 | async-start | bytes 22282240 | tf_op jit(solution)/shard_map/all_gather | solution.py:93
  197.9 95.8 %all-to-all-start = ((f32[256,16,384]{0,2,1:T(8,128)}), f32[256,16,384]{0,2,1:T(8,128)}, u32[]{:S(2)}, u32[]{:S(2)}) async-start(f32[256,16,384]{0,2,1:T(8,128)} %fusion.4), calls=%async_computation | async-start | bytes 12582912 | tf_op jit(solution)/shard_map/all_to_all | solution.py:101
  325.8 8.2 copy-start.2
  325.8 112.9 %all-to-all-start.1 = ((f32[8,768,384]{1,2,0:T(8,128)}), f32[8,768,384]{1,2,0:T(8,128)}, u32[]{:S(2)}, u32[]{:S(2)}) async-start(f32[8,768,384]{1,2,0:T(8,128)} %select_multiply_fusion), calls=%async_computation.1 | async-start | bytes 18874368 | tf_op jit(solution)/shard_map/all_to_all | solution.py:115
  333.6 3.2 copy-start.3
  333.6 318.3 %all-reduce.4.cloned.1.call-start = ((), (), s32[]{:S(2)}) async-start(), calls=%async_computation.2 | async-start | bytes 131072 | tf_op jit(solution)/shard_map/psum | solution.py:17
  334.1 14.9 %copy-start.6 = (s32[128]{0:T(128)S(1)}, s32[128]{0:T(128)}, u32[]{:S(2)}) copy-start(s32[128]{0:T(128)} %param.21) | copy-start | bytes 1540
  509.8 1.6 copy-start.5
  511.5 3.4 copy-start.4
  516.5 209.9 %all-reduce.8.cloned.1.call-start = ((), (), s32[]{:S(2)}) async-start(), calls=%async_computation.4 | async-start | bytes 1048576 | tf_op jit(solution)/shard_map/psum | solution.py:17
  670.5 145.5 %all-reduce.6.cloned.1.call-start = ((), (), s32[]{:S(2)}) async-start(), calls=%async_computation.3 | async-start | bytes 2097152 | tf_op jit(solution)/shard_map/psum | solution.py:17
  828.4 16.2 %copy-start.1 = (f32[1,256,1280]{2,1,0:T(8,128)S(1)}, f32[1,256,1280]{2,1,0:T(8,128)}, u32[]{:S(2)}) copy-start(f32[1,256,1280]{2,1,0:T(8,128)} %param.16) | copy-start | bytes 3932164
Sparse Core Ops, SparseCore 0:
  9.5 144.5 all-gather.2
  516.6 135.3 all-reduce.3
  670.6 55.7 all-reduce.7
  729.5 86.4 all-reduce.5

commit v2 on v1

v2 whole, which is shorter than its diff:
```python
import jax
import jax.numpy as jnp
from jax import lax
from jax.experimental import pallas as pl
from jax.experimental.pallas import tpu as pltpu
from jax.sharding import PartitionSpec as P

NB = 128
CB = 4096
PIV = 1280
NP = 16384
CHILDREN = 8
GROUPS = 16
RING = 4
CBT = CB // NB
PT = NP // NB
TR = PT // CHILDREN
TC = PT // GROUPS
COL_SLOTS = 3
ROW_SLOTS = 6
ROWS = CB // GROUPS
HALF = PIV // 2
QUARTER = PIV // 4
MESH = pl.DeviceIdType.MESH
ANY = pl.BlockSpec(memory_space=pl.ANY)
VMEM = pl.BlockSpec(memory_space=pltpu.VMEM)
SMEM = pl.BlockSpec(memory_space=pltpu.SMEM)


def full_dot(a, b):
    return jnp.dot(a, b, precision=lax.Precision.HIGHEST, preferred_element_type=jnp.float32)


def gather_kernel(pick_ref, front_hbm, left_hbm, right_hbm, by_column,
                  factors, front, left, contribution, chosen,
                  load_sem, ring_send, ring_recv, col_send, col_recv, own_sem):
    child = lax.axis_index("child")
    group = lax.axis_index("grp")
    at_y, at_x = group // RING, group % RING

    load_right = pltpu.make_async_copy(right_hbm, factors.at[group], load_sem.at[0])
    load_left = pltpu.make_async_copy(left_hbm, left, load_sem.at[1])
    load_front = pltpu.make_async_copy(front_hbm, front, load_sem.at[2])
    load_right.start()
    load_left.start()
    load_front.start()

    barrier = pltpu.get_barrier_semaphore()

    def greet(i, carry):
        pl.semaphore_signal(
            barrier, inc=1, device_id=(child, lax.rem(group + i, GROUPS)), device_id_type=MESH
        )
        return carry

    lax.fori_loop(1, GROUPS, greet, 0)
    pl.semaphore_wait(barrier, GROUPS - 1)

    def place(half, first, second):
        return second * RING + first if half == 0 else first * RING + second

    def turn(position, by):
        return lax.rem(position + by + RING, RING)

    def piece(half, block, quarter):
        if quarter is None:
            return factors.at[block, pl.ds(half * HALF, HALF)]
        return factors.at[block, pl.ds(half * HALF + quarter * QUARTER, QUARTER)]

    copies = {}

    def make(key, half, block, quarter, target):
        number = len(copies)
        ref = piece(half, block, quarter)
        copies[key] = pltpu.make_async_remote_copy(
            src_ref=ref, dst_ref=ref, send_sem=ring_send.at[number], recv_sem=ring_recv.at[number],
            device_id=(child, target), device_id_type=MESH,
        )

    lines = (0, -1, 1, 2)
    for half in (0, 1):
        first, second = (at_x, at_y) if half == 0 else (at_y, at_x)
        for way in (1, -1):
            target = place(half, turn(first, way), second)
            make((half, "a", way), half, place(half, first, second), None, target)
            make((half, "af", way), half, place(half, turn(first, -way), second),
                 0 if way == 1 else 1, target)
        for line in lines:
            column = turn(first, line)
            for way in (1, -1):
                target = place(half, first, turn(second, way))
                make((half, line, way), half, place(half, column, second), None, target)
                make((half, line, "f", way), half, place(half, column, turn(second, -way)),
                     0 if way == 1 else 1, target)

    def start(*key):
        for half in (0, 1):
            for way in (1, -1):
                copies[(half,) + key + (way,)].start()

    def arrive(*key):
        for half in (0, 1):
            for way in (1, -1):
                copies[(half,) + key + (way,)].wait_recv()

    def multiply(offsets):
        def one(i, carry):
            block = jnp.int32(0)
            for number, (dy, dx) in enumerate(offsets):
                block = jnp.where(i == number, turn(at_y, dy) * RING + turn(at_x, dx), block)
            product = full_dot(left[...], factors[block])
            base = pl.multiple_of(block * ROWS, ROWS)
            result = front[:, pl.ds(base, ROWS)] - product
            contribution[2 * block] = result[:, :NB]
            contribution[2 * block + 1] = result[:, NB:]
            return carry

        lax.fori_loop(0, len(offsets), one, 0)

    load_right.wait()
    start("a")
    start(0)
    load_left.wait()
    load_front.wait()
    multiply([(0, 0)])
    arrive("a")
    start("af")
    start(-1)
    start(1)
    arrive(0)
    start(0, "f")
    multiply([(0, 1), (0, -1), (1, 0), (-1, 0)])
    arrive("af")
    start(2)
    arrive(0, "f")
    multiply([(0, 2), (2, 0)])
    arrive(-1)
    start(-1, "f")
    arrive(1)
    start(1, "f")
    multiply([(1, 1), (1, -1), (-1, 1), (-1, -1)])
    arrive(2)
    start(2, "f")
    arrive(-1, "f")
    arrive(1, "f")
    multiply([(1, 2), (-1, 2), (2, 1), (2, -1)])
    arrive(2, "f")
    multiply([(2, 2)])

    def column_copy(slot, i):
        target = lax.rem(group + i, GROUPS)
        return pltpu.make_async_remote_copy(
            src_ref=chosen.at[slot, target],
            dst_ref=by_column.at[slot, pl.ds(2 * group, 2)],
            send_sem=col_send.at[slot * GROUPS + i], recv_sem=col_recv.at[slot * GROUPS + i],
            device_id=(child, target), device_id_type=MESH,
        )

    def own_copy(slot):
        return pltpu.make_async_copy(
            chosen.at[slot, group], by_column.at[slot, pl.ds(2 * group, 2)], own_sem.at[slot]
        )

    def select(slot, target):
        tile = contribution[pick_ref[target * COL_SLOTS + slot]]
        chosen[slot, target] = tile.reshape(2, NB, NB)

    for slot in range(COL_SLOTS):
        def send(i, carry):
            select(slot, lax.rem(group + i, GROUPS))
            column_copy(slot, i).start()
            return carry

        lax.fori_loop(1, GROUPS, send, 0)
        select(slot, group)
        own_copy(slot).start()

    for key in copies:
        copies[key].wait_send()
    for slot in range(COL_SLOTS):
        def finish(i, carry):
            column_copy(slot, i).wait_recv()
            column_copy(slot, i).wait_send()
            return carry

        lax.fori_loop(1, GROUPS, finish, 0)
        own_copy(slot).wait()


def gather_columns(pick, front, left, right):
    return pl.pallas_call(
        gather_kernel,
        out_shape=jax.ShapeDtypeStruct((COL_SLOTS, CBT, NB, NB), jnp.float32),
        in_specs=[SMEM, ANY, ANY, ANY],
        out_specs=ANY,
        scratch_shapes=[
            pltpu.VMEM((GROUPS, PIV, ROWS), jnp.float32),
            pltpu.VMEM((ROWS, CB), jnp.float32),
            pltpu.VMEM((ROWS, PIV), jnp.float32),
            pltpu.VMEM((CBT, ROWS, NB), jnp.float32),
            pltpu.VMEM((COL_SLOTS, GROUPS, 2, NB, NB), jnp.float32),
            pltpu.SemaphoreType.DMA((3,)),
            pltpu.SemaphoreType.DMA((40,)),
            pltpu.SemaphoreType.DMA((40,)),
            pltpu.SemaphoreType.DMA((COL_SLOTS * GROUPS,)),
            pltpu.SemaphoreType.DMA((COL_SLOTS * GROUPS,)),
            pltpu.SemaphoreType.DMA((COL_SLOTS,)),
        ],
        compiler_params=pltpu.CompilerParams(
            collective_id=0, has_side_effects=True, vmem_limit_bytes=52 * 2**20
        ),
        name="gather_columns",
    )(pick, front, left, right)


def factor_tile(packed_ref, lower_ref, upper_ref):
    rows = lax.broadcasted_iota(jnp.int32, (NB, NB), 0)
    cols = lax.broadcasted_iota(jnp.int32, (NB, NB), 1)
    lane = lax.broadcasted_iota(jnp.int32, (1, NB), 1)
    eye = jnp.where(rows == cols, 1.0, 0.0)
    lower_ref[...] = eye
    upper_ref[...] = eye

    def eliminate(j, carry):
        working = packed_ref[...]
        upper = upper_ref[...]
        row_part = packed_ref[pl.ds(j, 1), :]
        row_lower = lower_ref[pl.ds(j, 1), :]
        column = jnp.sum(jnp.where(cols == j, working, 0.0), axis=1, keepdims=True)
        column_upper = jnp.sum(jnp.where(cols == j, upper, 0.0), axis=1, keepdims=True)
        pivot_value = jnp.sum(jnp.where(lane == j, row_part, 0.0), axis=1, keepdims=True)
        multiplier = jnp.where(rows[:, :1] > j, column / pivot_value, 0.0)
        right = jnp.where(lane > j, row_part, 0.0)
        packed_ref[...] = jnp.where(
            (cols == j) & (rows > j), multiplier, working - multiplier * right
        )
        lower_ref[...] = lower_ref[...] - multiplier * row_lower
        scaled = column_upper / pivot_value
        upper_ref[...] = jnp.where(cols == j, scaled, upper - scaled * right)
        return carry

    lax.fori_loop(0, NB, eliminate, 0)


def row_kernel(pick_ref, lead_ref, row_slot_ref, by_column, lead_block, lead_diag, pivots,
               arrived, left_panel, top_parts, packed, lower, upper,
               chosen, first_column, raw_lead,
               top_send, top_recv, row_send, row_recv, own_sem, lead_send, lead_recv,
               load_sem, spread_send, spread_recv, share_send, share_recv):
    child = lax.axis_index("child")
    group = lax.axis_index("grp")

    barrier = pltpu.get_barrier_semaphore()

    def greet_group(i, carry):
        pl.semaphore_signal(
            barrier, inc=1, device_id=(child, lax.rem(group + i, GROUPS)), device_id_type=MESH
        )
        return carry

    def greet_child(i, carry):
        pl.semaphore_signal(
            barrier, inc=1, device_id=(lax.rem(child + i, CHILDREN), group), device_id_type=MESH
        )
        return carry

    lax.fori_loop(1, GROUPS, greet_group, 0)
    lax.fori_loop(1, CHILDREN, greet_child, 0)
    pl.semaphore_wait(barrier, GROUPS + CHILDREN - 2)

    def top_copy(i):
        return pltpu.make_async_remote_copy(
            src_ref=top_parts.at[child], dst_ref=top_parts.at[child],
            send_sem=top_send.at[i], recv_sem=top_recv.at[i],
            device_id=(lax.rem(child + i, CHILDREN), group), device_id_type=MESH,
        )

    for slot in range(COL_SLOTS):
        top_parts[child, slot] = by_column[slot, pick_ref[0]]

    def send_top(i, carry):
        top_copy(i).start()
        return carry

    lax.fori_loop(1, CHILDREN, send_top, 0)

    def row_copy(slot, i):
        target = lax.rem(child + i, CHILDREN)
        return pltpu.make_async_remote_copy(
            src_ref=chosen.at[slot, target], dst_ref=arrived.at[slot, child],
            send_sem=row_send.at[slot * CHILDREN + i], recv_sem=row_recv.at[slot * CHILDREN + i],
            device_id=(target, group), device_id_type=MESH,
        )

    def own_copy(slot):
        return pltpu.make_async_copy(
            chosen.at[slot, child], arrived.at[slot, child], own_sem.at[slot]
        )

    def select(slot, target):
        for r in range(ROW_SLOTS):
            chosen[slot, target, r] = by_column[slot, pick_ref[target * ROW_SLOTS + r]]

    for slot in range(COL_SLOTS):
        def send(i, carry):
            select(slot, lax.rem(child + i, CHILDREN))
            row_copy(slot, i).start()
            return carry

        lax.fori_loop(1, CHILDREN, send, 0)
        select(slot, child)
        own_copy(slot).start()

    def arrive_top(i, carry):
        top_copy(i).wait_recv()
        return carry

    lax.fori_loop(1, CHILDREN, arrive_top, 0)

    def lead_copy(target):
        return pltpu.make_async_remote_copy(
            src_ref=raw_lead, dst_ref=raw_lead,
            send_sem=lead_send.at[target], recv_sem=lead_recv.at[0],
            device_id=(child, target), device_id_type=MESH,
        )

    rows = lax.broadcasted_iota(jnp.int32, (NB, NB), 0)
    cols = lax.broadcasted_iota(jnp.int32, (NB, NB), 1)

    @pl.when(group == 0)
    def _():
        total = lead_block[...] + jnp.where(rows == cols, lead_diag[...], 0.0)
        for k in range(CHILDREN):
            total = total + jnp.where(lead_ref[k] > 0, top_parts[k, 0], 0.0)
        chosen_rows = jnp.where(pivots[...] == cols, 1.0, 0.0)
        raw_lead[...] = full_dot(chosen_rows, total)

        def send_lead(i, carry):
            lead_copy(i).start()
            return carry

        lax.fori_loop(1, GROUPS, send_lead, 0)

    @pl.when(group != 0)
    def _():
        lead_copy(0).wait_recv()

    packed[...] = raw_lead[...]
    factor_tile(packed, lower, upper)

    def finish_rows(slot):
        def finish(i, carry):
            row_copy(slot, i).wait_recv()
            row_copy(slot, i).wait_send()
            return carry

        lax.fori_loop(1, CHILDREN, finish, 0)
        own_copy(slot).wait()

    def spread_copy(target):
        return pltpu.make_async_remote_copy(
            src_ref=left_panel.at[target], dst_ref=left_panel.at[target],
            send_sem=spread_send.at[target], recv_sem=spread_recv.at[0],
            device_id=(child, target), device_id_type=MESH,
        )

    def own_spread():
        return pltpu.make_async_remote_copy(
            src_ref=left_panel.at[group], dst_ref=left_panel.at[group],
            send_sem=spread_send.at[0], recv_sem=spread_recv.at[0],
            device_id=(child, 0), device_id_type=MESH,
        )

    def share_copy(i):
        return pltpu.make_async_remote_copy(
            src_ref=left_panel.at[group], dst_ref=left_panel.at[group],
            send_sem=share_send.at[i], recv_sem=share_recv.at[i],
            device_id=(child, lax.rem(group + i, GROUPS)), device_id_type=MESH,
        )

    finish_rows(0)

    @pl.when(group == 0)
    def _():
        load = pltpu.make_async_copy(arrived.at[0], first_column, load_sem.at[0])
        load.start()
        load.wait()

        def assemble(i, carry):
            a = lax.rem(i, TR)
            total = jnp.zeros((NB, NB), jnp.float32)
            for k in range(CHILDREN):
                slot = row_slot_ref[k * TR + a]
                held = (slot >= 0) & (lead_ref[k] > 0)
                tile = first_column[k, jnp.maximum(slot, 0)]
                total = total + jnp.where(held, tile, 0.0)
            left_panel[a] = total

            @pl.when(a > 0)
            def _():
                spread_copy(a).start()

            return carry

        lax.fori_loop(1, TR + 1, assemble, 0)

    @pl.when(group != 0)
    def _():
        own_spread().wait_recv()

    def send_share(i, carry):
        @pl.when(lax.rem(group + i, GROUPS) != 0)
        def _():
            share_copy(i).start()
        return carry

    lax.fori_loop(1, GROUPS, send_share, 0)

    def finish_top(i, carry):
        top_copy(i).wait_send()
        return carry

    lax.fori_loop(1, CHILDREN, finish_top, 0)

    def finish_share(i, carry):
        @pl.when(lax.rem(group + i, GROUPS) != 0)
        def _():
            share_copy(i).wait_send()

        @pl.when(group != 0)
        def _():
            share_copy(i).wait_recv()

        @pl.when(group == 0)
        def _():
            lead_copy(i).wait_send()
            spread_copy(i).wait_send()

        return carry

    lax.fori_loop(1, GROUPS, finish_share, 0)
    finish_rows(1)
    finish_rows(2)


def exchange_rows(pick, lead_held, row_slot, by_column, lead_block, lead_diag, pivots):
    tile = jax.ShapeDtypeStruct((NB, NB), jnp.float32)
    return pl.pallas_call(
        row_kernel,
        out_shape=(
            jax.ShapeDtypeStruct((COL_SLOTS, CHILDREN, ROW_SLOTS, NB, NB), jnp.float32),
            jax.ShapeDtypeStruct((TR, NB, NB), jnp.float32),
            jax.ShapeDtypeStruct((CHILDREN, COL_SLOTS, NB, NB), jnp.float32),
            tile, tile, tile,
        ),
        in_specs=[SMEM, SMEM, SMEM, VMEM, VMEM, VMEM, VMEM],
        out_specs=(ANY, VMEM, VMEM, VMEM, VMEM, VMEM),
        scratch_shapes=[
            pltpu.VMEM((COL_SLOTS, CHILDREN, ROW_SLOTS, NB, NB), jnp.float32),
            pltpu.VMEM((CHILDREN, ROW_SLOTS, NB, NB), jnp.float32),
            pltpu.VMEM((NB, NB), jnp.float32),
            pltpu.SemaphoreType.DMA((CHILDREN,)),
            pltpu.SemaphoreType.DMA((CHILDREN,)),
            pltpu.SemaphoreType.DMA((COL_SLOTS * CHILDREN,)),
            pltpu.SemaphoreType.DMA((COL_SLOTS * CHILDREN,)),
            pltpu.SemaphoreType.DMA((COL_SLOTS,)),
            pltpu.SemaphoreType.DMA((GROUPS,)),
            pltpu.SemaphoreType.DMA((1,)),
            pltpu.SemaphoreType.DMA((1,)),
            pltpu.SemaphoreType.DMA((GROUPS,)),
            pltpu.SemaphoreType.DMA((1,)),
            pltpu.SemaphoreType.DMA((GROUPS,)),
            pltpu.SemaphoreType.DMA((GROUPS,)),
        ],
        compiler_params=pltpu.CompilerParams(
            collective_id=1, has_side_effects=True, vmem_limit_bytes=52 * 2**20
        ),
        name="exchange_rows",
    )(pick, lead_held, row_slot, by_column, lead_block, lead_diag, pivots)


def update_kernel(place_ref, lead_ref, row_slot_ref, col_slot_ref, arrived, left_raw, top_parts,
                  packed, lower, upper, diag, pivots, out_ref, right):
    a = pl.program_id(0)
    child, group = place_ref[0], place_ref[1]
    rows = lax.broadcasted_iota(jnp.int32, (NB, NB), 0)
    cols = lax.broadcasted_iota(jnp.int32, (NB, NB), 1)

    @pl.when(a == 0)
    def _():
        right[...] = jnp.zeros_like(right)
        for k in range(CHILDREN):
            for b in range(TC):
                slot = col_slot_ref[k * TC + b]

                @pl.when((slot >= 0) & (lead_ref[k] > 0))
                def _():
                    span = pl.ds(b * NB, NB)
                    right[:, span] = right[:, span] + top_parts[k, slot]

        chosen_rows = jnp.where(pivots[...] == cols, 1.0, 0.0)
        right[...] = full_dot(lower[...], full_dot(chosen_rows, right[...]))

        @pl.when(group == 0)
        def _():
            right[:, :NB] = jnp.zeros((NB, NB), jnp.float32)

    top = (a == 0) & (child == 0)

    @pl.when(top)
    def _():
        out_ref[...] = right[...]

        @pl.when(group == 0)
        def _():
            out_ref[:, :NB] = packed[...]

    @pl.when(jnp.logical_not(top))
    def _():
        left = full_dot(left_raw[0], upper[...])
        out_ref[...] = -full_dot(left, right[...])
        for k in range(CHILDREN):
            row_slot = row_slot_ref[k * TR + a]

            @pl.when(row_slot >= 0)
            def _():
                for b in range(TC):
                    col_slot = col_slot_ref[k * TC + b]

                    @pl.when(col_slot >= 0)
                    def _():
                        span = pl.ds(b * NB, NB)
                        out_ref[:, span] = out_ref[:, span] + arrived[col_slot, k, row_slot]

        on_diag = (lax.rem(group, CHILDREN) == child) & (lax.rem(a, 2) == group // CHILDREN)

        @pl.when(on_diag)
        def _():
            span = pl.ds(pl.multiple_of((a // 2) * NB, NB), NB)
            out_ref[:, span] = out_ref[:, span] + jnp.where(rows == cols, diag[0], 0.0)

        @pl.when(group == 0)
        def _():
            out_ref[:, :NB] = left


def update_front(place, lead_held, row_slot, col_slot, arrived, left_raw, top_parts,
                 packed, lower, upper, diag, pivots):
    return pl.pallas_call(
        update_kernel,
        grid=(TR,),
        out_shape=jax.ShapeDtypeStruct((TR * NB, TC * NB), jnp.float32),
        in_specs=[
            SMEM, SMEM, SMEM, SMEM, VMEM,
            pl.BlockSpec((1, NB, NB), lambda a: (a, 0, 0)),
            VMEM, VMEM, VMEM, VMEM,
            pl.BlockSpec((1, 1, NB), lambda a: (a, 0, 0)),
            VMEM,
        ],
        out_specs=pl.BlockSpec((NB, TC * NB), lambda a: (a, 0)),
        scratch_shapes=[pltpu.VMEM((NB, TC * NB), jnp.float32)],
        compiler_params=pltpu.CompilerParams(vmem_limit_bytes=52 * 2**20),
        name="update_front",
    )(place, lead_held, row_slot, col_slot, arrived, left_raw, top_parts,
      packed, lower, upper, diag, pivots)


def slot_tables(child_map):
    tiles = jnp.arange(PT)
    hits = child_map[:, None, :] == tiles[None, :, None]
    present = jnp.any(hits, axis=2)
    source = jnp.sum(jnp.where(hits, jnp.arange(CBT)[None, None, :], 0), axis=2)

    def by_class(classes, capacity):
        count = PT // classes
        held = present.reshape(CHILDREN, count, classes).transpose(0, 2, 1)
        tile = source.reshape(CHILDREN, count, classes).transpose(0, 2, 1)
        earlier = jnp.arange(count)[None, :] < jnp.arange(count)[:, None]
        rank = jnp.sum((held[:, :, None, :] & earlier).astype(jnp.int32), axis=3)
        slot = jnp.where(held, rank, -1)
        wanted = slot[:, :, None, :] == jnp.arange(capacity)[None, None, :, None]
        pick = jnp.sum(jnp.where(wanted, tile[:, :, None, :], 0), axis=3)
        return slot, pick

    return present, by_class(GROUPS, COL_SLOTS), by_class(CHILDREN, ROW_SLOTS)


def body(front_child, left_factor, right_factor, child_map, parent_diag, lead_block, pivots):
    child = lax.axis_index("child")
    group = lax.axis_index("grp")
    present, (col_slot, col_pick), (row_slot, row_pick) = slot_tables(child_map)

    def mine(table, index, dim):
        return lax.dynamic_index_in_dim(table, index, dim, keepdims=False).reshape(-1)

    lead_held = present[:, 0].astype(jnp.int32)
    row_slots = mine(row_slot, child, 1)
    col_slots = mine(col_slot, group, 1)
    pivot_column = pivots.reshape(NB, 1)
    by_column = gather_columns(
        mine(col_pick, child, 0), front_child[0], left_factor[0], right_factor[0]
    )
    arrived, left_raw, top_parts, packed, lower, upper = exchange_rows(
        mine(row_pick, child, 0), lead_held, row_slots, by_column, lead_block,
        parent_diag[:NB].reshape(1, NB), pivot_column,
    )
    diag = lax.dynamic_index_in_dim(
        parent_diag.reshape(TR, CHILDREN, NB), child, 1, keepdims=True
    )
    front = update_front(
        jnp.stack([child, group]).astype(jnp.int32), lead_held, row_slots, col_slots,
        arrived, left_raw, top_parts, packed, lower, upper, diag, pivot_column,
    )
    return front.reshape(1, TR * NB, 1, TC * NB)


def solution(mesh):
    in_specs = (
        P("child", "grp", None),
        P("child", "grp", None),
        P("child", None, "grp"),
        P(),
        P(),
        P(),
        P(),
    )
    out_specs = P("child", None, "grp", None)
    return jax.shard_map(body, mesh=mesh, in_specs=in_specs, out_specs=out_specs, check_vma=False)
```

time: 853 us -> 368 us (0.43)
  waiting for transfers between devices: 598 us -> 0 us
  Pallas kernels: 16.2 us -> 348 us
  local copies, waits for them, and re-layouts: 101 us -> 15.8 us
  matrix products: 83 us -> 0 us
  other arithmetic: 26.4 us -> 4.08 us
  between operations: 13.5 us -> 0.14 us
  starting transfers between devices: 12.6 us -> 0 us
    pallas_call x1 -> x3, Pallas kernels: 16.2 us -> 348 us  [the longest x1 192 us: gather_columns(): pl.pallas_call(gather_kernel, out_shape=jax.ShapeDtypeStruct((COL_SLOTS,...]
    psum x3 -> x0, waiting for transfers between devices: 276 us -> none  [from_root(): return lax.psum(jnp.where(mine, shard, jnp.zeros_like(shard)), axis)]
    all_to_all x2 -> x0, waiting for transfers between devices: 178 us -> none  [the longest x1 89.3 us: body(): lax.all_to_all(second, 'child', split_axis=0, concat_axis=0, tiled=True)]
    all_gather x1 -> x0, waiting for transfers between devices: 144 us -> none  [body(): lax.all_gather(local_right, 'grp', axis=1, tiled=True)]
    dot_general x6 -> x0, matrix products: 83 us -> none  [the longest x1 28.4 us: body(): jnp.einsum('kaisj,kbs->aibj', placed, col_hot, precision=full_precision)]
    gather x14 -> x0, local copies, waits for them, and re-layouts: 44.4 us -> none  [the longest x2 17.2 us: body(): jnp.take(by_column, row_pick.reshape(-1), axis=0)]
    scatter x1 -> x0, local copies, waits for them, and re-layouts: 16.1 us -> none  [body(): updated.at[:NB, :].set(jnp.where(is_first_row, top_out, updated[:NB, :]))]
    mul x4 -> x0, other arithmetic: 16 us -> none  [the longest x1 8.39 us: body(): jnp.take(by_column, row_pick.reshape(-1), axis=0)]
  transfers between devices with their start and end apart: 6 -> 0, of which waited for: 6 -> 0; matrix products, arithmetic and copies ran while one was open for 3% -> 0% of each run, Pallas kernels for 0% -> 0%
where the time goes in v2:
time: 368 us
  Pallas kernels  348 us (95%)
  local copies, waits for them, and re-layouts  15.8 us (4%)
  other arithmetic  4.08 us (1%)
    pallas_call x1, Pallas kernels, gather_columns(): pl.pallas_call(gather_kernel, out_shape=jax.ShapeDtypeStruct((COL_SLOTS,...  192 us
    pallas_call x1, Pallas kernels, exchange_rows(): pl.pallas_call(row_kernel, out_shape=(jax.ShapeDtypeStruct((COL_SLOTS, CH...  132 us
    pallas_call x1, Pallas kernels, update_front(): pl.pallas_call(update_kernel, grid=(TR,), out_shape=jax.ShapeDtypeStruct(...  24.1 us
    reshape x1, local copies, waits for them, and re-layouts, body(): return front.reshape(1, TR * NB, 1, TC * NB)  10.8 us

profile of v2, /device:TPU:1, one launch (start us, length us, event | category | flops | bytes accessed | tf_op | source)
XLA Modules:
  0.0 368.1 jit_solution(10890582447410277632)
XLA Ops:
  0.0 0.1 pad_add_fusion.place_ref
  0.1 0.7 slice_bitcast_fusion.lead_diag
  0.8 0.8 fusion
  1.6 0.1 convert_reduce_fusion.2.lead_ref
  1.7 0.8 select_reduce_fusion.1
  2.5 0.1 reshape.75
  2.6 0.9 constant_dynamic-slice_fusion.diag
  3.4 0.1 reshape.73
  3.5 0.1 copy.34
  3.6 1.2 convert_reduce_fusion
  4.9 0.1 reshape.74.row_slot_ref
  4.9 0.2 convert_reduce_fusion.1
  5.1 0.3 dynamic-slice_reduce_fusion
  5.4 0.1 reshape.76.col_slot_ref
  5.5 0.1 reshape.79
  5.6 0.1 select_reduce_fusion.2
  5.6 0.1 copy.37
  5.7 0.1 reshape.80.pick_ref
  5.8 0.1 reshape.77
  5.9 0.1 copy.35
  6.0 0.9 select_reduce_fusion
  6.9 0.1 copy.36
  7.0 0.1 reshape.78.pick_ref
  7.0 0.8 copy.38.pivots
  7.8 0.0 copy-start
  7.8 1.3 copy-done
  9.1 0.0 copy-start.1
  9.1 191.6 %gather_columns.1.by_column = f32[3,32,128,128]{3,2,1,0:T(8,128)} custom-call(s32[48]{0:T(128)S(1)} %reshape.80.pick_ref, f32[256,4096]{1,0:T(8,128)} %bitcast.18, f32[256,1280]{1,0:T(8,128)S(1)} %bitcast.16, f32[1280,256]{1,0:T(8,128)} %bitcast.19), custom_call_target="tpu_custom_call" | custom-call | tf_op jit(solution)/shard_map/gather_columns/pallas_call | solution.py:191
  200.7 0.0 copy-done.1
  200.7 132.4 %exchange_rows.1 = (f32[3,8,6,128,128]{4,3,2,1,0:T(8,128)}, f32[16,128,128]{2,1,0:T(8,128)S(1)}, f32[8,3,128,128]{3,2,1,0:T(8,128)}, f32[128,128]{1,0:T(8,128)S(...) custom-call(s32[48]{0:T(128)S(1)} %reshape.78.pick_ref, s32[8]{0:T(128)S(1)} %convert_reduce_fusion.2.lead_ref, ...), custom_call_target="tpu_custom_call" | custom-call | tf_op jit(solution)/shard_map/exchange_rows/pallas_call | solution.py:448
  333.1 24.1 %update_front.1 = f32[2048,1024]{1,0:T(8,128)} custom-call(s32[2]{0:T(128)S(1)} %pad_add_fusion.place_ref, s32[8]{0:T(128)S(1)} %convert_reduce_fusion.2.lead_ref, s32[128]{0:T(128)S(1)} %reshape.74.row_slot_ref, s32[64]{0:T(128)S(1)} %reshape.76.col_slot_ref, f32[3,8,6,128,128]{4,3,2,1,0:T(8,128)} %get-tuple-element.11.arrived, ...), custom_call_target="tpu_custom_call" | custom-call | tf_op jit(solution)/shard_map/update_front/pallas_call | solution.py:549
  357.2 10.8 %copy.40 = f32[1,2048,1,1024]{3,2,1,0:T(1,128)} copy(f32[1,2048,1,1024]{3,1,2,0:T(8,128)} %bitcast.17) | data formatting | bytes 16777216 | tf_op jit(solution)/shard_map/reshape | solution.py:614
  (7 shorter events, 0.1 us)
Async XLA Ops:
  7.8 1.3 copy-start
  9.1 191.6 %copy-start.1 = (f32[128,128]{1,0:T(8,128)S(1)}, f32[128,128]{1,0:T(8,128)}, u32[]{:S(2)}) copy-start(f32[128,128]{1,0:T(8,128)} %lead_block.1) | copy-start | bytes 196612

commit v3 on v2

--- a/solution.py
+++ b/solution.py
@@ -31,9 +31,43 @@
     return jnp.dot(a, b, precision=lax.Precision.HIGHEST, preferred_element_type=jnp.float32)
 
 
-def gather_kernel(pick_ref, front_hbm, left_hbm, right_hbm, by_column,
-                  factors, front, left, contribution, chosen,
-                  load_sem, ring_send, ring_recv, col_send, col_recv, own_sem):
+def factor_tile(packed_ref, lower_ref, upper_ref):
+    rows = lax.broadcasted_iota(jnp.int32, (NB, NB), 0)
+    cols = lax.broadcasted_iota(jnp.int32, (NB, NB), 1)
+    lane = lax.broadcasted_iota(jnp.int32, (1, NB), 1)
+    eye = jnp.where(rows == cols, 1.0, 0.0)
+    lower_ref[...] = eye
+    upper_ref[...] = eye
+
+    def eliminate(j, carry):
+        working = packed_ref[...]
+        upper = upper_ref[...]
+        row_part = packed_ref[pl.ds(j, 1), :]
+        row_lower = lower_ref[pl.ds(j, 1), :]
+        column = jnp.sum(jnp.where(cols == j, working, 0.0), axis=1, keepdims=True)
+        column_upper = jnp.sum(jnp.where(cols == j, upper, 0.0), axis=1, keepdims=True)
+        pivot_value = jnp.sum(jnp.where(lane == j, row_part, 0.0), axis=1, keepdims=True)
+        multiplier = jnp.where(rows[:, :1] > j, column / pivot_value, 0.0)
+        right = jnp.where(lane > j, row_part, 0.0)
+        packed_ref[...] = jnp.where(
+            (cols == j) & (rows > j), multiplier, working - multiplier * right
+        )
+        lower_ref[...] = lower_ref[...] - multiplier * row_lower
+        scaled = column_upper / pivot_value
+        upper_ref[...] = jnp.where(cols == j, scaled, upper - scaled * right)
+        return carry
+
+    lax.fori_loop(0, NB, eliminate, 0)
+
+
+def exchange_kernel(col_pick_ref, row_pick_ref, lead_ref, row_slot_ref,
+                    front_hbm, left_hbm, right_hbm, lead_block, lead_diag, pivots,
+                    arrived, left_panel, top_parts, packed, lower, upper,
+                    factors, front, left, contribution, col_chosen, column_0, column_1, column_2,
+                    first_column, raw_lead,
+                    load_sem, ring_send, ring_recv, col_send, col_recv, own_col_sem,
+                    top_send, top_recv, row_send, row_recv, own_row_sem, lead_send, lead_recv,
+                    spread_send, spread_recv, share_send, share_recv):
     child = lax.axis_index("child")
     group = lax.axis_index("grp")
     at_y, at_x = group // RING, group % RING
@@ -47,14 +81,21 @@
 
     barrier = pltpu.get_barrier_semaphore()
 
-    def greet(i, carry):
+    def greet_group(i, carry):
         pl.semaphore_signal(
             barrier, inc=1, device_id=(child, lax.rem(group + i, GROUPS)), device_id_type=MESH
         )
         return carry
 
-    lax.fori_loop(1, GROUPS, greet, 0)
-    pl.semaphore_wait(barrier, GROUPS - 1)
+    def greet_child(i, carry):
+        pl.semaphore_signal(
+            barrier, inc=1, device_id=(lax.rem(child + i, CHILDREN), group), device_id_type=MESH
+        )
+        return carry
+
+    lax.fori_loop(1, GROUPS, greet_group, 0)
+    lax.fori_loop(1, CHILDREN, greet_child, 0)
+    pl.semaphore_wait(barrier, GROUPS + CHILDREN - 2)
 
     def place(half, first, second):
         return second * RING + first if half == 0 else first * RING + second
@@ -147,175 +188,110 @@
     arrive(2, "f")
     multiply([(2, 2)])
 
+    by_column = (column_0, column_1, column_2)
+
     def column_copy(slot, i):
         target = lax.rem(group + i, GROUPS)
         return pltpu.make_async_remote_copy(
-            src_ref=chosen.at[slot, target],
-            dst_ref=by_column.at[slot, pl.ds(2 * group, 2)],
+            src_ref=col_chosen.at[slot, target],
+            dst_ref=by_column[slot].at[pl.ds(2 * group, 2)],
             send_sem=col_send.at[slot * GROUPS + i], recv_sem=col_recv.at[slot * GROUPS + i],
             device_id=(child, target), device_id_type=MESH,
         )
 
-    def own_copy(slot):
+    def own_column_copy(slot):
         return pltpu.make_async_copy(
-            chosen.at[slot, group], by_column.at[slot, pl.ds(2 * group, 2)], own_sem.at[slot]
-        )
-
-    def select(slot, target):
-        tile = contribution[pick_ref[target * COL_SLOTS + slot]]
-        chosen[slot, target] = tile.reshape(2, NB, NB)
+            col_chosen.at[slot, group], by_column[slot].at[pl.ds(2 * group, 2)],
+            own_col_sem.at[slot],
+        )
+
+    def select_column(slot, target):
+        tile = contribution[col_pick_ref[target * COL_SLOTS + slot]]
+        col_chosen[slot, target] = tile.reshape(2, NB, NB)
 
     for slot in range(COL_SLOTS):
-        def send(i, carry):
-            select(slot, lax.rem(group + i, GROUPS))
+        def send_column(i, carry):
+            select_column(slot, lax.rem(group + i, GROUPS))
             column_copy(slot, i).start()
             return carry
 
-        lax.fori_loop(1, GROUPS, send, 0)
-        select(slot, group)
-        own_copy(slot).start()
+        lax.fori_loop(1, GROUPS, send_column, 0)
+        select_column(slot, group)
+        own_column_copy(slot).start()
 
     for key in copies:
         copies[key].wait_send()
-    for slot in range(COL_SLOTS):
-        def finish(i, carry):
-            column_copy(slot, i).wait_recv()
-            column_copy(slot, i).wait_send()
-            return carry
-
-        lax.fori_loop(1, GROUPS, finish, 0)
-        own_copy(slot).wait()
-
-
-def gather_columns(pick, front, left, right):
-    return pl.pallas_call(
-        gather_kernel,
-        out_shape=jax.ShapeDtypeStruct((COL_SLOTS, CBT, NB, NB), jnp.float32),
-        in_specs=[SMEM, ANY, ANY, ANY],
-        out_specs=ANY,
-        scratch_shapes=[
-            pltpu.VMEM((GROUPS, PIV, ROWS), jnp.float32),
-            pltpu.VMEM((ROWS, CB), jnp.float32),
-            pltpu.VMEM((ROWS, PIV), jnp.float32),
-            pltpu.VMEM((CBT, ROWS, NB), jnp.float32),
-            pltpu.VMEM((COL_SLOTS, GROUPS, 2, NB, NB), jnp.float32),
-            pltpu.SemaphoreType.DMA((3,)),
-            pltpu.SemaphoreType.DMA((40,)),
-            pltpu.SemaphoreType.DMA((40,)),
-            pltpu.SemaphoreType.DMA((COL_SLOTS * GROUPS,)),
-            pltpu.SemaphoreType.DMA((COL_SLOTS * GROUPS,)),
-            pltpu.SemaphoreType.DMA((COL_SLOTS,)),
-        ],
-        compiler_params=pltpu.CompilerParams(
-            collective_id=0, has_side_effects=True, vmem_limit_bytes=52 * 2**20
-        ),
-        name="gather_columns",
-    )(pick, front, left, right)
-
-
-def factor_tile(packed_ref, lower_ref, upper_ref):
-    rows = lax.broadcasted_iota(jnp.int32, (NB, NB), 0)
-    cols = lax.broadcasted_iota(jnp.int32, (NB, NB), 1)
-    lane = lax.broadcasted_iota(jnp.int32, (1, NB), 1)
-    eye = jnp.where(rows == cols, 1.0, 0.0)
-    lower_ref[...] = eye
-    upper_ref[...] = eye
-
-    def eliminate(j, carry):
-        working = packed_ref[...]
-        upper = upper_ref[...]
-        row_part = packed_ref[pl.ds(j, 1), :]
-        row_lower = lower_ref[pl.ds(j, 1), :]
-        column = jnp.sum(jnp.where(cols == j, working, 0.0), axis=1, keepdims=True)
-        column_upper = jnp.sum(jnp.where(cols == j, upper, 0.0), axis=1, keepdims=True)
-        pivot_value = jnp.sum(jnp.where(lane == j, row_part, 0.0), axis=1, keepdims=True)
-        multiplier = jnp.where(rows[:, :1] > j, column / pivot_value, 0.0)
-        right = jnp.where(lane > j, row_part, 0.0)
-        packed_ref[...] = jnp.where(
-            (cols == j) & (rows > j), multiplier, working - multiplier * right
-        )
-        lower_ref[...] = lower_ref[...] - multiplier * row_lower
-        scaled = column_upper / pivot_value
-        upper_ref[...] = jnp.where(cols == j, scaled, upper - scaled * right)
-        return carry
-
-    lax.fori_loop(0, NB, eliminate, 0)
-
-
-def row_kernel(pick_ref, lead_ref, row_slot_ref, by_column, lead_block, lead_diag, pivots,
-               arrived, left_panel, top_parts, packed, lower, upper,
-               chosen, first_column, raw_lead,
-               top_send, top_recv, row_send, row_recv, own_sem, lead_send, lead_recv,
-               load_sem, spread_send, spread_recv, share_send, share_recv):
-    child = lax.axis_index("child")
-    group = lax.axis_index("grp")
-
-    barrier = pltpu.get_barrier_semaphore()
-
-    def greet_group(i, carry):
-        pl.semaphore_signal(
-            barrier, inc=1, device_id=(child, lax.rem(group + i, GROUPS)), device_id_type=MESH
-        )
-        return carry
-
-    def greet_child(i, carry):
-        pl.semaphore_signal(
-            barrier, inc=1, device_id=(lax.rem(child + i, CHILDREN), group), device_id_type=MESH
-        )
-        return carry
-
-    lax.fori_loop(1, GROUPS, greet_group, 0)
-    lax.fori_loop(1, CHILDREN, greet_child, 0)
-    pl.semaphore_wait(barrier, GROUPS + CHILDREN - 2)
-
-    def top_copy(i):
+
+    def top_copy(slot, i):
         return pltpu.make_async_remote_copy(
-            src_ref=top_parts.at[child], dst_ref=top_parts.at[child],
-            send_sem=top_send.at[i], recv_sem=top_recv.at[i],
+            src_ref=top_parts.at[child, slot], dst_ref=top_parts.at[child, slot],
+            send_sem=top_send.at[slot * CHILDREN + i], recv_sem=top_recv.at[slot * CHILDREN + i],
             device_id=(lax.rem(child + i, CHILDREN), group), device_id_type=MESH,
         )
 
-    for slot in range(COL_SLOTS):
-        top_parts[child, slot] = by_column[slot, pick_ref[0]]
-
-    def send_top(i, carry):
-        top_copy(i).start()
-        return carry
-
-    lax.fori_loop(1, CHILDREN, send_top, 0)
+    def row_buffer(slot, target):
+        number = slot * CHILDREN + target
+        lanes = pl.multiple_of(lax.rem(number, 2) * NB, NB)
+        return factors.at[number // 2, pl.ds(0, ROW_SLOTS * NB), pl.ds(lanes, NB)]
 
     def row_copy(slot, i):
         target = lax.rem(child + i, CHILDREN)
         return pltpu.make_async_remote_copy(
-            src_ref=chosen.at[slot, target], dst_ref=arrived.at[slot, child],
+            src_ref=row_buffer(slot, target), dst_ref=arrived.at[slot, child],
             send_sem=row_send.at[slot * CHILDREN + i], recv_sem=row_recv.at[slot * CHILDREN + i],
             device_id=(target, group), device_id_type=MESH,
         )
 
-    def own_copy(slot):
+    def own_row_copy(slot):
         return pltpu.make_async_copy(
-            chosen.at[slot, child], arrived.at[slot, child], own_sem.at[slot]
-        )
-
-    def select(slot, target):
+            row_buffer(slot, child), arrived.at[slot, child], own_row_sem.at[slot]
+        )
+
+    def select_rows(slot, target):
+        number = slot * CHILDREN + target
+        lanes = pl.multiple_of(lax.rem(number, 2) * NB, NB)
         for r in range(ROW_SLOTS):
-            chosen[slot, target, r] = by_column[slot, pick_ref[target * ROW_SLOTS + r]]
-
-    for slot in range(COL_SLOTS):
-        def send(i, carry):
-            select(slot, lax.rem(child + i, CHILDREN))
+            tile = by_column[slot][row_pick_ref[target * ROW_SLOTS + r]]
+            factors[number // 2, pl.ds(r * NB, NB), pl.ds(lanes, NB)] = tile
+
+    def pass_rows(slot):
+        def finish(i, carry):
+            column_copy(slot, i).wait_recv()
+            return carry
+
+        lax.fori_loop(1, GROUPS, finish, 0)
+        own_column_copy(slot).wait()
+        top_parts[child, slot] = by_column[slot][row_pick_ref[0]]
+
+        def send_top(i, carry):
+            top_copy(slot, i).start()
+            return carry
+
+        lax.fori_loop(1, CHILDREN, send_top, 0)
+
+        def send_rows(i, carry):
+            select_rows(slot, lax.rem(child + i, CHILDREN))
             row_copy(slot, i).start()
             return carry
 
-        lax.fori_loop(1, CHILDREN, send, 0)
-        select(slot, child)
-        own_copy(slot).start()
-
-    def arrive_top(i, carry):
-        top_copy(i).wait_recv()
-        return carry
-
-    lax.fori_loop(1, CHILDREN, arrive_top, 0)
+        lax.fori_loop(1, CHILDREN, send_rows, 0)
+        select_rows(slot, child)
+        own_row_copy(slot).start()
+
+    def finish_top(slot):
+        def arrive_top(i, carry):
+            top_copy(slot, i).wait_recv()
+            return carry
+
+        lax.fori_loop(1, CHILDREN, arrive_top, 0)
+
+    def finish_rows(slot):
+        def finish(i, carry):
+            row_copy(slot, i).wait_recv()
+            return carry
+
+        lax.fori_loop(1, CHILDREN, finish, 0)
+        own_row_copy(slot).wait()
 
     def lead_copy(target):
         return pltpu.make_async_remote_copy(
@@ -324,6 +300,29 @@
             device_id=(child, target), device_id_type=MESH,
         )
 
+    def spread_copy(target):
+        return pltpu.make_async_remote_copy(
+            src_ref=left_panel.at[target], dst_ref=left_panel.at[target],
+            send_sem=spread_send.at[target], recv_sem=spread_recv.at[0],
+            device_id=(child, target), device_id_type=MESH,
+        )
+
+    def own_spread():
+        return pltpu.make_async_remote_copy(
+            src_ref=left_panel.at[group], dst_ref=left_panel.at[group],
+            send_sem=spread_send.at[0], recv_sem=spread_recv.at[0],
+            device_id=(child, 0), device_id_type=MESH,
+        )
+
+    def share_copy(i):
+        return pltpu.make_async_remote_copy(
+            src_ref=left_panel.at[group], dst_ref=left_panel.at[group],
+            send_sem=share_send.at[i], recv_sem=share_recv.at[i],
+            device_id=(child, lax.rem(group + i, GROUPS)), device_id_type=MESH,
+        )
+
+    pass_rows(0)
+    finish_top(0)
     rows = lax.broadcasted_iota(jnp.int32, (NB, NB), 0)
     cols = lax.broadcasted_iota(jnp.int32, (NB, NB), 1)
 
@@ -341,50 +340,30 @@
 
         lax.fori_loop(1, GROUPS, send_lead, 0)
 
+    pass_rows(1)
+
     @pl.when(group != 0)
     def _():
         lead_copy(0).wait_recv()
 
     packed[...] = raw_lead[...]
     factor_tile(packed, lower, upper)
-
-    def finish_rows(slot):
-        def finish(i, carry):
-            row_copy(slot, i).wait_recv()
-            row_copy(slot, i).wait_send()
-            return carry
-
-        lax.fori_loop(1, CHILDREN, finish, 0)
-        own_copy(slot).wait()
-
-    def spread_copy(target):
-        return pltpu.make_async_remote_copy(
-            src_ref=left_panel.at[target], dst_ref=left_panel.at[target],
-            send_sem=spread_send.at[target], recv_sem=spread_recv.at[0],
-            device_id=(child, target), device_id_type=MESH,
-        )
-
-    def own_spread():
-        return pltpu.make_async_remote_copy(
-            src_ref=left_panel.at[group], dst_ref=left_panel.at[group],
-            send_sem=spread_send.at[0], recv_sem=spread_recv.at[0],
-            device_id=(child, 0), device_id_type=MESH,
-        )
-
-    def share_copy(i):
-        return pltpu.make_async_remote_copy(
-            src_ref=left_panel.at[group], dst_ref=left_panel.at[group],
-            send_sem=share_send.at[i], recv_sem=share_recv.at[i],
-            device_id=(child, lax.rem(group + i, GROUPS)), device_id_type=MESH,
-        )
+    pass_rows(2)
 
     finish_rows(0)
 
     @pl.when(group == 0)
     def _():
-        load = pltpu.make_async_copy(arrived.at[0], first_column, load_sem.at[0])
-        load.start()
-        load.wait()
+        loads = [
+            pltpu.make_async_copy(
+                arrived.at[0, :, pl.ds(r * NB, NB), :], first_column.at[:, r], load_sem.at[r]
+            )
+            for r in range(ROW_SLOTS)
+        ]
+        for load in loads:
+            load.start()
+        for load in loads:
+            load.wait()
 
         def assemble(i, carry):
             a = lax.rem(i, TR)
@@ -415,12 +394,8 @@
         return carry
 
     lax.fori_loop(1, GROUPS, send_share, 0)
-
-    def finish_top(i, carry):
-        top_copy(i).wait_send()
-        return carry
-
-    lax.fori_loop(1, CHILDREN, finish_top, 0)
+    finish_top(1)
+    finish_top(2)
 
     def finish_share(i, carry):
         @pl.when(lax.rem(group + i, GROUPS) != 0)
@@ -442,41 +417,56 @@
     finish_rows(1)
     finish_rows(2)
 
-
-def exchange_rows(pick, lead_held, row_slot, by_column, lead_block, lead_diag, pivots):
+    for slot in range(COL_SLOTS):
+        def sent_columns(i, carry):
+            column_copy(slot, i).wait_send()
+            return carry
+
+        def sent_rows(i, carry):
+            top_copy(slot, i).wait_send()
+            row_copy(slot, i).wait_send()
+            return carry
+
+        lax.fori_loop(1, GROUPS, sent_columns, 0)
+        lax.fori_loop(1, CHILDREN, sent_rows, 0)
+
+
+def exchange(col_pick, row_pick, lead_held, row_slot, front, left, right,
+             lead_block, lead_diag, pivots):
     tile = jax.ShapeDtypeStruct((NB, NB), jnp.float32)
+    dma = pltpu.SemaphoreType.DMA
     return pl.pallas_call(
-        row_kernel,
+        exchange_kernel,
         out_shape=(
-            jax.ShapeDtypeStruct((COL_SLOTS, CHILDREN, ROW_SLOTS, NB, NB), jnp.float32),
+            jax.ShapeDtypeStruct((COL_SLOTS, CHILDREN, ROW_SLOTS * NB, NB), jnp.float32),
             jax.ShapeDtypeStruct((TR, NB, NB), jnp.float32),
             jax.ShapeDtypeStruct((CHILDREN, COL_SLOTS, NB, NB), jnp.float32),
             tile, tile, tile,
         ),
-        in_specs=[SMEM, SMEM, SMEM, VMEM, VMEM, VMEM, VMEM],
+        in_specs=[SMEM, SMEM, SMEM, SMEM, ANY, ANY, ANY, VMEM, VMEM, VMEM],
         out_specs=(ANY, VMEM, VMEM, VMEM, VMEM, VMEM),
         scratch_shapes=[
-            pltpu.VMEM((COL_SLOTS, CHILDREN, ROW_SLOTS, NB, NB), jnp.float32),
+            pltpu.VMEM((GROUPS, PIV, ROWS), jnp.float32),
+            pltpu.VMEM((ROWS, CB), jnp.float32),
+            pltpu.VMEM((ROWS, PIV), jnp.float32),
+            pltpu.VMEM((CBT, ROWS, NB), jnp.float32),
+            pltpu.VMEM((COL_SLOTS, GROUPS, 2, NB, NB), jnp.float32),
+            pltpu.VMEM((CBT, NB, NB), jnp.float32),
+            pltpu.VMEM((CBT, NB, NB), jnp.float32),
+            pltpu.VMEM((CBT, NB, NB), jnp.float32),
             pltpu.VMEM((CHILDREN, ROW_SLOTS, NB, NB), jnp.float32),
             pltpu.VMEM((NB, NB), jnp.float32),
-            pltpu.SemaphoreType.DMA((CHILDREN,)),
-            pltpu.SemaphoreType.DMA((CHILDREN,)),
-            pltpu.SemaphoreType.DMA((COL_SLOTS * CHILDREN,)),
-            pltpu.SemaphoreType.DMA((COL_SLOTS * CHILDREN,)),
-            pltpu.SemaphoreType.DMA((COL_SLOTS,)),
-            pltpu.SemaphoreType.DMA((GROUPS,)),
-            pltpu.SemaphoreType.DMA((1,)),
-            pltpu.SemaphoreType.DMA((1,)),
-            pltpu.SemaphoreType.DMA((GROUPS,)),
-            pltpu.SemaphoreType.DMA((1,)),
-            pltpu.SemaphoreType.DMA((GROUPS,)),
-            pltpu.SemaphoreType.DMA((GROUPS,)),
+            dma((ROW_SLOTS,)), dma((40,)), dma((40,)),
+            dma((COL_SLOTS * GROUPS,)), dma((COL_SLOTS * GROUPS,)), dma((COL_SLOTS,)),
+            dma((COL_SLOTS * CHILDREN,)), dma((COL_SLOTS * CHILDREN,)),
+            dma((COL_SLOTS * CHILDREN,)), dma((COL_SLOTS * CHILDREN,)), dma((COL_SLOTS,)),
+            dma((GROUPS,)), dma((1,)), dma((GROUPS,)), dma((1,)), dma((GROUPS,)), dma((GROUPS,)),
         ],
         compiler_params=pltpu.CompilerParams(
-            collective_id=1, has_side_effects=True, vmem_limit_bytes=52 * 2**20
+            collective_id=0, has_side_effects=True, vmem_limit_bytes=56 * 2**20
         ),
-        name="exchange_rows",
-    )(pick, lead_held, row_slot, by_column, lead_block, lead_diag, pivots)
+        name="exchange",
+    )(col_pick, row_pick, lead_held, row_slot, front, left, right, lead_block, lead_diag, pivots)
 
 
 def update_kernel(place_ref, lead_ref, row_slot_ref, col_slot_ref, arrived, left_raw, top_parts,
@@ -524,13 +514,14 @@
 
             @pl.when(row_slot >= 0)
             def _():
+                base = pl.multiple_of(row_slot * NB, NB)
                 for b in range(TC):
                     col_slot = col_slot_ref[k * TC + b]
 
                     @pl.when(col_slot >= 0)
                     def _():
                         span = pl.ds(b * NB, NB)
-                        out_ref[:, span] = out_ref[:, span] + arrived[col_slot, k, row_slot]
+                        out_ref[:, span] = out_ref[:, span] + arrived[col_slot, k, pl.ds(base, NB), :]
 
         on_diag = (lax.rem(group, CHILDREN) == child) & (lax.rem(a, 2) == group // CHILDREN)
 
@@ -597,11 +588,9 @@
     row_slots = mine(row_slot, child, 1)
     col_slots = mine(col_slot, group, 1)
     pivot_column = pivots.reshape(NB, 1)
-    by_column = gather_columns(
-        mine(col_pick, child, 0), front_child[0], left_factor[0], right_factor[0]
-    )
-    arrived, left_raw, top_parts, packed, lower, upper = exchange_rows(
-        mine(row_pick, child, 0), lead_held, row_slots, by_column, lead_block,
+    arrived, left_raw, top_parts, packed, lower, upper = exchange(
+        mine(col_pick, child, 0), mine(row_pick, child, 0), lead_held, row_slots,
+        front_child[0], left_factor[0], right_factor[0], lead_block,
         parent_diag[:NB].reshape(1, NB), pivot_column,
     )
     diag = lax.dynamic_index_in_dim(

time: 368 us -> 324 us (0.88)
  Pallas kernels: 348 us -> 296 us
  local copies, waits for them, and re-layouts: 15.8 us -> 20.9 us
    pallas_call x2 -> x1, Pallas kernels: 324 us -> 272 us  [exchange(): pl.pallas_call(exchange_kernel, out_shape=(jax.ShapeDtypeStruct((COL_SLOT...]
where the time goes in v3:
time: 324 us; the launch traced here: 321 us
  Pallas kernels  296 us (91%)
  local copies, waits for them, and re-layouts  20.9 us (6%)
  other arithmetic  4.56 us (1%)
    pallas_call x1, Pallas kernels, exchange(): pl.pallas_call(exchange_kernel, out_shape=(jax.ShapeDtypeStruct((COL_SLOT...  272 us
    pallas_call x1, Pallas kernels, update_front(): pl.pallas_call(update_kernel, grid=(TR,), out_shape=jax.ShapeDtypeStruct(...  24.1 us
    reshape x1, local copies, waits for them, and re-layouts, body(): return front.reshape(1, TR * NB, 1, TC * NB)  10.8 us

profile of v3, /device:TPU:1, one launch (start us, length us, event | category | flops | bytes accessed | tf_op | source)
XLA Modules:
  0.0 321.4 jit_solution(16121832609483745749)
XLA Ops:
  0.0 0.1 pad_add_fusion.place_ref
  0.1 1.2 slice_bitcast_fusion.lead_diag
  1.3 0.8 fusion
  2.1 0.6 convert_reduce_fusion.2.lead_ref
  2.7 0.0 copy-start.6
  2.7 0.8 select_reduce_fusion.1
  3.5 0.1 reshape.75
  3.6 0.9 constant_dynamic-slice_fusion.diag
  4.4 0.1 reshape.73
  4.5 0.1 copy.34
  4.6 1.2 convert_reduce_fusion
  5.8 0.6 reshape.74.row_slot_ref
  6.5 0.0 copy-start.5
  6.5 0.1 convert_reduce_fusion.1
  6.6 0.3 dynamic-slice_reduce_fusion
  6.9 0.1 reshape.76.col_slot_ref
  7.0 0.1 reshape.77
  7.1 0.1 select_reduce_fusion.2
  7.1 0.1 copy.35
  7.2 0.6 reshape.78.col_pick_ref
  7.8 0.1 reshape.79
  7.9 0.1 copy.36
  8.0 0.9 select_reduce_fusion
  8.9 0.1 copy.37
  9.0 0.6 reshape.80.row_pick_ref
  9.6 1.4 copy.38.pivots
  11.0 0.0 copy-start.1
  11.0 271.7 %exchange.1 = (f32[3,8,768,128]{3,2,1,0:T(8,128)}, f32[16,128,128]{2,1,0:T(8,128)}, f32[8,3,128,128]{3,2,1,0:T(8,128)}, f32[128,128]{1,0:T(8,128)}, f32[128,128]{1,0:T(8,128)}, /*index=5*/f32[128,128]{1,0:T(8,128)}) custom-call(s32[48]{0:T(128)} %reshape.78.col_pick_ref, s32[48]{0:T(128)} %reshape.80.row_pick_ref, s32[8]{0:T(128)} %convert_reduce_fusion.2.lead_ref, ...), custom_call_target="tpu_custom_call" | custom-call | tf_op jit(solution)/shard_map/exchange/pallas_call | solution.py:438
  282.7 0.0 copy-done.6
  282.7 0.0 copy-done.5
  282.7 0.0 copy-done.1
  282.8 0.0 copy-start
  282.8 1.2 copy-done
  284.0 0.0 copy-start.2
  284.0 0.8 copy-done.2
  284.8 0.0 copy-start.3
  284.8 0.8 copy-done.3
  285.7 0.0 copy-start.4
  285.7 0.8 copy-done.4
  286.5 24.1 %update_front.1 = f32[2048,1024]{1,0:T(8,128)} custom-call(s32[2]{0:T(128)S(1)} %pad_add_fusion.place_ref, s32[8]{0:T(128)S(1)} %copy-done.6, s32[128]{0:T(128)S(1)} %copy-done.5, s32[64]{0:T(128)S(1)} %reshape.76.col_slot_ref, f32[3,8,768,128]{3,2,1,0:T(8,128)} %get-tuple-element.11.arrived, f32[16,128,128]{2,1,0:T(8,128)S(1)} %copy-done, ...), custom_call_target="tpu_custom_call" | custom-call | tf_op jit(solution)/shard_map/update_front/pallas_call | solution.py:540
  310.6 10.8 %copy.40 = f32[1,2048,1,1024]{3,2,1,0:T(1,128)} copy(f32[1,2048,1,1024]{3,1,2,0:T(8,128)} %bitcast.16) | data formatting | bytes 16777216 | tf_op jit(solution)/shard_map/reshape | solution.py:603
  (7 shorter events, 0.1 us)
Async XLA Ops:
  2.7 280.1 %copy-start.6 = (s32[8]{0:T(128)S(1)}, s32[8]{0:T(128)}, u32[]{:S(2)}) copy-start(s32[8]{0:T(128)} %convert_reduce_fusion.2.lead_ref) | copy-start | bytes 100
  6.5 276.3 %copy-start.5 = (s32[128]{0:T(128)S(1)}, s32[128]{0:T(128)}, u32[]{:S(2)}) copy-start(s32[128]{0:T(128)} %reshape.74.row_slot_ref) | copy-start | bytes 1540
  11.0 271.7 %copy-start.1 = (s32[128,1]{1,0:T(8,128)S(1)}, s32[128,1]{1,0:T(8,128)}, u32[]{:S(2)}) copy-start(s32[128,1]{1,0:T(8,128)} %copy.38.pivots) | copy-start | bytes 1540
  282.8 1.2 copy-start
  284.0 0.8 copy-start.2
  284.8 0.8 copy-start.3
  285.7 0.8 copy-start.4

commit v4 on v3

--- a/solution.py
+++ b/solution.py
@@ -19,6 +19,11 @@
 COL_SLOTS = 3
 ROW_SLOTS = 6
 ROWS = CB // GROUPS
+COL_SLOT = 0
+ROW_SLOT = CHILDREN
+COL_PICK = 2 * CHILDREN
+ROW_PICK = COL_PICK + COL_SLOTS * CHILDREN
+TABLE_ROWS = ROW_PICK + ROW_SLOTS * CHILDREN
 HALF = PIV // 2
 QUARTER = PIV // 4
 MESH = pl.DeviceIdType.MESH
@@ -29,6 +34,50 @@
 
 def full_dot(a, b):
     return jnp.dot(a, b, precision=lax.Precision.HIGHEST, preferred_element_type=jnp.float32)
+
+
+def table_kernel(map_ref, table_ref):
+    lanes = lax.broadcasted_iota(jnp.int32, (CHILDREN, PT), 1)
+    tiles = map_ref[...]
+    source = jnp.full((CHILDREN, PT), -1, jnp.int32)
+    for t in range(CBT):
+        source = jnp.where(tiles[:, t:t + 1] == lanes, t, source)
+    held = (source >= 0).astype(jnp.int32)
+
+    def fill(classes, capacity, slot_base, pick_base):
+        rank = jnp.zeros((CHILDREN, PT), jnp.int32)
+        for shift in range(classes, PT, classes):
+            rank = rank + jnp.where(lanes >= shift, pltpu.roll(held, shift, 1), 0)
+        slots = jnp.where(held > 0, rank, -1)
+        table_ref[slot_base:slot_base + CHILDREN] = slots
+        for slot in range(capacity):
+            picked = jnp.where(slots == slot, source, 0)
+            shift = classes
+            while shift < PT:
+                picked = picked + pltpu.roll(picked, shift, 1)
+                shift *= 2
+            base = pick_base + slot * CHILDREN
+            table_ref[base:base + CHILDREN] = picked
+
+    fill(GROUPS, COL_SLOTS, COL_SLOT, COL_PICK)
+    fill(CHILDREN, ROW_SLOTS, ROW_SLOT, ROW_PICK)
+
+
+def slot_table(child_map):
+    return pl.pallas_call(
+        table_kernel,
+        out_shape=jax.ShapeDtypeStruct((TABLE_ROWS, PT), jnp.int32),
+        name="slot_table",
+    )(child_map)
+
+
+def permute_rows(pivots, values):
+    rows = lax.broadcasted_iota(jnp.int32, (NB, NB), 0)
+    chosen = jnp.where(rows == pivots[...], 1.0, 0.0)
+    return lax.dot_general(
+        chosen, values, (((0,), (0,)), ((), ())),
+        precision=lax.Precision.HIGHEST, preferred_element_type=jnp.float32,
+    )
 
 
 def factor_tile(packed_ref, lower_ref, upper_ref):
@@ -60,8 +109,7 @@
     lax.fori_loop(0, NB, eliminate, 0)
 
 
-def exchange_kernel(col_pick_ref, row_pick_ref, lead_ref, row_slot_ref,
-                    front_hbm, left_hbm, right_hbm, lead_block, lead_diag, pivots,
+def exchange_kernel(table_ref, front_hbm, left_hbm, right_hbm, lead_block, diag, pivots,
                     arrived, left_panel, top_parts, packed, lower, upper,
                     factors, front, left, contribution, col_chosen, column_0, column_1, column_2,
                     first_column, raw_lead,
@@ -190,8 +238,11 @@
 
     by_column = (column_0, column_1, column_2)
 
+    def column_target(i):
+        return lax.rem(group + i, GROUPS)
+
     def column_copy(slot, i):
-        target = lax.rem(group + i, GROUPS)
+        target = column_target(i)
         return pltpu.make_async_remote_copy(
             src_ref=col_chosen.at[slot, target],
             dst_ref=by_column[slot].at[pl.ds(2 * group, 2)],
@@ -206,18 +257,22 @@
         )
 
     def select_column(slot, target):
-        tile = contribution[col_pick_ref[target * COL_SLOTS + slot]]
+        tile = contribution[table_ref[COL_PICK + slot * CHILDREN + child, target]]
         col_chosen[slot, target] = tile.reshape(2, NB, NB)
 
-    for slot in range(COL_SLOTS):
+    def pass_columns(slot):
         def send_column(i, carry):
-            select_column(slot, lax.rem(group + i, GROUPS))
+            select_column(slot, column_target(i))
             column_copy(slot, i).start()
             return carry
 
         lax.fori_loop(1, GROUPS, send_column, 0)
         select_column(slot, group)
         own_column_copy(slot).start()
+
+    pass_columns(0)
+    pass_columns(1)
+    pass_columns(2)
 
     for key in copies:
         copies[key].wait_send()
@@ -251,7 +306,7 @@
         number = slot * CHILDREN + target
         lanes = pl.multiple_of(lax.rem(number, 2) * NB, NB)
         for r in range(ROW_SLOTS):
-            tile = by_column[slot][row_pick_ref[target * ROW_SLOTS + r]]
+            tile = by_column[slot][table_ref[ROW_PICK + r * CHILDREN + child, target]]
             factors[number // 2, pl.ds(r * NB, NB), pl.ds(lanes, NB)] = tile
 
     def pass_rows(slot):
@@ -261,7 +316,7 @@
 
         lax.fori_loop(1, GROUPS, finish, 0)
         own_column_copy(slot).wait()
-        top_parts[child, slot] = by_column[slot][row_pick_ref[0]]
+        top_parts[child, slot] = by_column[slot][table_ref[ROW_PICK + child, 0]]
 
         def send_top(i, carry):
             top_copy(slot, i).start()
@@ -328,11 +383,10 @@
 
     @pl.when(group == 0)
     def _():
-        total = lead_block[...] + jnp.where(rows == cols, lead_diag[...], 0.0)
+        total = lead_block[...] + jnp.where(rows == cols, diag[0:1, :], 0.0)
         for k in range(CHILDREN):
-            total = total + jnp.where(lead_ref[k] > 0, top_parts[k, 0], 0.0)
-        chosen_rows = jnp.where(pivots[...] == cols, 1.0, 0.0)
-        raw_lead[...] = full_dot(chosen_rows, total)
+            total = total + jnp.where(table_ref[COL_SLOT + k, 0] >= 0, top_parts[k, 0], 0.0)
+        raw_lead[...] = permute_rows(pivots, total)
 
         def send_lead(i, carry):
             lead_copy(i).start()
@@ -369,8 +423,8 @@
             a = lax.rem(i, TR)
             total = jnp.zeros((NB, NB), jnp.float32)
             for k in range(CHILDREN):
-                slot = row_slot_ref[k * TR + a]
-                held = (slot >= 0) & (lead_ref[k] > 0)
+                slot = table_ref[ROW_SLOT + k, a * CHILDREN + child]
+                held = (slot >= 0) & (table_ref[COL_SLOT + k, 0] >= 0)
                 tile = first_column[k, jnp.maximum(slot, 0)]
                 total = total + jnp.where(held, tile, 0.0)
             left_panel[a] = total
@@ -431,8 +485,7 @@
         lax.fori_loop(1, CHILDREN, sent_rows, 0)
 
 
-def exchange(col_pick, row_pick, lead_held, row_slot, front, left, right,
-             lead_block, lead_diag, pivots):
+def exchange(table, front, left, right, lead_block, diag, pivots):
     tile = jax.ShapeDtypeStruct((NB, NB), jnp.float32)
     dma = pltpu.SemaphoreType.DMA
     return pl.pallas_call(
@@ -443,7 +496,7 @@
             jax.ShapeDtypeStruct((CHILDREN, COL_SLOTS, NB, NB), jnp.float32),
             tile, tile, tile,
         ),
-        in_specs=[SMEM, SMEM, SMEM, SMEM, ANY, ANY, ANY, VMEM, VMEM, VMEM],
+        in_specs=[SMEM, ANY, ANY, ANY, VMEM, VMEM, VMEM],
         out_specs=(ANY, VMEM, VMEM, VMEM, VMEM, VMEM),
         scratch_shapes=[
             pltpu.VMEM((GROUPS, PIV, ROWS), jnp.float32),
@@ -466,13 +519,19 @@
             collective_id=0, has_side_effects=True, vmem_limit_bytes=56 * 2**20
         ),
         name="exchange",
-    )(col_pick, row_pick, lead_held, row_slot, front, left, right, lead_block, lead_diag, pivots)
-
-
-def update_kernel(place_ref, lead_ref, row_slot_ref, col_slot_ref, arrived, left_raw, top_parts,
-                  packed, lower, upper, diag, pivots, out_ref, right):
+    )(table, front, left, right, lead_block, diag, pivots)
+
+
+def split(values):
+    high = values.astype(jnp.bfloat16)
+    return high, (values - high.astype(jnp.float32)).astype(jnp.bfloat16)
+
+
+def update_kernel(table_ref, arrived, left_raw, top_parts,
+                  packed, lower, upper, diag, pivots, out_ref, right, right_parts, total):
     a = pl.program_id(0)
-    child, group = place_ref[0], place_ref[1]
+    child = lax.axis_index("child")
+    group = lax.axis_index("grp")
     rows = lax.broadcasted_iota(jnp.int32, (NB, NB), 0)
     cols = lax.broadcasted_iota(jnp.int32, (NB, NB), 1)
 
@@ -481,126 +540,104 @@
         right[...] = jnp.zeros_like(right)
         for k in range(CHILDREN):
             for b in range(TC):
-                slot = col_slot_ref[k * TC + b]
-
-                @pl.when((slot >= 0) & (lead_ref[k] > 0))
+                slot = table_ref[COL_SLOT + k, b * GROUPS + group]
+
+                @pl.when((slot >= 0) & (table_ref[COL_SLOT + k, 0] >= 0))
                 def _():
                     span = pl.ds(b * NB, NB)
                     right[:, span] = right[:, span] + top_parts[k, slot]
 
-        chosen_rows = jnp.where(pivots[...] == cols, 1.0, 0.0)
-        right[...] = full_dot(lower[...], full_dot(chosen_rows, right[...]))
+        right[...] = full_dot(lower[...], permute_rows(pivots, right[...]))
 
         @pl.when(group == 0)
         def _():
             right[:, :NB] = jnp.zeros((NB, NB), jnp.float32)
+
+        high, low = split(right[...])
+        right_parts[0:NB] = high
+        right_parts[NB:2 * NB] = low
+        right_parts[2 * NB:] = high
 
     top = (a == 0) & (child == 0)
 
     @pl.when(top)
     def _():
-        out_ref[...] = right[...]
+        total[...] = right[...]
 
         @pl.when(group == 0)
         def _():
-            out_ref[:, :NB] = packed[...]
+            total[:, :NB] = packed[...]
 
     @pl.when(jnp.logical_not(top))
     def _():
         left = full_dot(left_raw[0], upper[...])
-        out_ref[...] = -full_dot(left, right[...])
+        high, low = split(left)
+        left_parts = jnp.concatenate([high, high, low], axis=1)
+        total[...] = -jnp.dot(
+            left_parts, right_parts[...], preferred_element_type=jnp.float32
+        )
         for k in range(CHILDREN):
-            row_slot = row_slot_ref[k * TR + a]
+            row_slot = table_ref[ROW_SLOT + k, a * CHILDREN + child]
 
             @pl.when(row_slot >= 0)
             def _():
                 base = pl.multiple_of(row_slot * NB, NB)
                 for b in range(TC):
-                    col_slot = col_slot_ref[k * TC + b]
+                    col_slot = table_ref[COL_SLOT + k, b * GROUPS + group]
 
                     @pl.when(col_slot >= 0)
                     def _():
                         span = pl.ds(b * NB, NB)
-                        out_ref[:, span] = out_ref[:, span] + arrived[col_slot, k, pl.ds(base, NB), :]
+                        total[:, span] = total[:, span] + arrived[col_slot, k, pl.ds(base, NB), :]
 
         on_diag = (lax.rem(group, CHILDREN) == child) & (lax.rem(a, 2) == group // CHILDREN)
 
         @pl.when(on_diag)
         def _():
             span = pl.ds(pl.multiple_of((a // 2) * NB, NB), NB)
-            out_ref[:, span] = out_ref[:, span] + jnp.where(rows == cols, diag[0], 0.0)
+            entries = diag[pl.ds(a * CHILDREN + child, 1), :]
+            total[:, span] = total[:, span] + jnp.where(rows == cols, entries, 0.0)
 
         @pl.when(group == 0)
         def _():
-            out_ref[:, :NB] = left
-
-
-def update_front(place, lead_held, row_slot, col_slot, arrived, left_raw, top_parts,
+            total[:, :NB] = left
+
+    out_ref[0, :, 0, :] = total[...]
+
+
+def update_front(table, arrived, left_raw, top_parts,
                  packed, lower, upper, diag, pivots):
     return pl.pallas_call(
         update_kernel,
         grid=(TR,),
-        out_shape=jax.ShapeDtypeStruct((TR * NB, TC * NB), jnp.float32),
+        out_shape=jax.ShapeDtypeStruct((1, TR * NB, 1, TC * NB), jnp.float32),
         in_specs=[
-            SMEM, SMEM, SMEM, SMEM, VMEM,
+            SMEM, VMEM,
             pl.BlockSpec((1, NB, NB), lambda a: (a, 0, 0)),
-            VMEM, VMEM, VMEM, VMEM,
-            pl.BlockSpec((1, 1, NB), lambda a: (a, 0, 0)),
-            VMEM,
+            VMEM, VMEM, VMEM, VMEM, VMEM, VMEM,
         ],
-        out_specs=pl.BlockSpec((NB, TC * NB), lambda a: (a, 0)),
-        scratch_shapes=[pltpu.VMEM((NB, TC * NB), jnp.float32)],
-        compiler_params=pltpu.CompilerParams(vmem_limit_bytes=52 * 2**20),
+        out_specs=pl.BlockSpec((1, NB, 1, TC * NB), lambda a: (0, a, 0, 0)),
+        scratch_shapes=[
+            pltpu.VMEM((NB, TC * NB), jnp.float32),
+            pltpu.VMEM((3 * NB, TC * NB), jnp.bfloat16),
+            pltpu.VMEM((NB, TC * NB), jnp.float32),
+        ],
+        compiler_params=pltpu.CompilerParams(vmem_limit_bytes=60 * 2**20),
         name="update_front",
-    )(place, lead_held, row_slot, col_slot, arrived, left_raw, top_parts,
+    )(table, arrived, left_raw, top_parts,
       packed, lower, upper, diag, pivots)
 
 
-def slot_tables(child_map):
-    tiles = jnp.arange(PT)
-    hits = child_map[:, None, :] == tiles[None, :, None]
-    present = jnp.any(hits, axis=2)
-    source = jnp.sum(jnp.where(hits, jnp.arange(CBT)[None, None, :], 0), axis=2)
-
-    def by_class(classes, capacity):
-        count = PT // classes
-        held = present.reshape(CHILDREN, count, classes).transpose(0, 2, 1)
-        tile = source.reshape(CHILDREN, count, classes).transpose(0, 2, 1)
-        earlier = jnp.arange(count)[None, :] < jnp.arange(count)[:, None]
-        rank = jnp.sum((held[:, :, None, :] & earlier).astype(jnp.int32), axis=3)
-        slot = jnp.where(held, rank, -1)
-        wanted = slot[:, :, None, :] == jnp.arange(capacity)[None, None, :, None]
-        pick = jnp.sum(jnp.where(wanted, tile[:, :, None, :], 0), axis=3)
-        return slot, pick
-
-    return present, by_class(GROUPS, COL_SLOTS), by_class(CHILDREN, ROW_SLOTS)
-
-
 def body(front_child, left_factor, right_factor, child_map, parent_diag, lead_block, pivots):
-    child = lax.axis_index("child")
-    group = lax.axis_index("grp")
-    present, (col_slot, col_pick), (row_slot, row_pick) = slot_tables(child_map)
-
-    def mine(table, index, dim):
-        return lax.dynamic_index_in_dim(table, index, dim, keepdims=False).reshape(-1)
-
-    lead_held = present[:, 0].astype(jnp.int32)
-    row_slots = mine(row_slot, child, 1)
-    col_slots = mine(col_slot, group, 1)
-    pivot_column = pivots.reshape(NB, 1)
+    diag = parent_diag.reshape(PT, NB)
+    pivot_row = pivots.reshape(1, NB)
+    table = slot_table(child_map)
     arrived, left_raw, top_parts, packed, lower, upper = exchange(
-        mine(col_pick, child, 0), mine(row_pick, child, 0), lead_held, row_slots,
-        front_child[0], left_factor[0], right_factor[0], lead_block,
-        parent_diag[:NB].reshape(1, NB), pivot_column,
+        table, front_child[0], left_factor[0], right_factor[0], lead_block, diag, pivot_row
     )
-    diag = lax.dynamic_index_in_dim(
-        parent_diag.reshape(TR, CHILDREN, NB), child, 1, keepdims=True
+    return update_front(
+        table, arrived, left_raw, top_parts, packed, lower, upper, diag, pivot_row
     )
-    front = update_front(
-        jnp.stack([child, group]).astype(jnp.int32), lead_held, row_slots, col_slots,
-        arrived, left_raw, top_parts, packed, lower, upper, diag, pivot_column,
-    )
-    return front.reshape(1, TR * NB, 1, TC * NB)
 
 
 def solution(mesh):

time: 324 us -> 299 us (0.923)
  local copies, waits for them, and re-layouts: 20.9 us -> 0 us
  other arithmetic: 4.56 us -> 0 us
    reshape x12 -> x0, local copies, waits for them, and re-layouts: 15.8 us -> none  [the longest x1 10.8 us: body(): return front.reshape(1, TR * NB, 1, TC * NB)]
    unnamed x14 -> x0, local copies, waits for them, and re-layouts: 3.75 us -> none
where the time goes in v4:
time: 299 us; the launch traced here: 296 us
  Pallas kernels  296 us (99%)
    pallas_call x1, Pallas kernels, exchange(): pl.pallas_call(exchange_kernel, out_shape=(jax.ShapeDtypeStruct((COL_SLOT...  272 us
    pallas_call x1, Pallas kernels, update_front(): pl.pallas_call(update_kernel, grid=(TR,), out_shape=jax.ShapeDtypeStruct(...  22.3 us

profile of v4, /device:TPU:1, one launch (start us, length us, event | category | flops | bytes accessed | tf_op | source)
XLA Modules:
  0.0 296.5 jit_solution(15033139383305254506)
XLA Ops:
  0.0 1.8 slot_table.1.table_ref
  1.8 272.3 %exchange.1 = (f32[3,8,768,128]{3,2,1,0:T(8,128)}, f32[16,128,128]{2,1,0:T(8,128)}, f32[8,3,128,128]{3,2,1,0:T(8,128)}, f32[128,128]{1,0:T(8,128)}, f32[128,128]{1,0:T(8,128)}, /*index=5*/f32[128,128]{1,0:T(8,128)}) custom-call(s32[88,128]{1,0:T(8,128)} %slot_table.1.table_ref, f32[256,4096]{1,0:T(8,128)} %bitcast.5, f32[256,1280]{1,0:T(8,128)} %bitcast.6, ...), custom_call_target="tpu_custom_call" | custom-call | tf_op jit(solution)/shard_map/exchange/pallas_call | solution.py:491
  274.1 22.3 %update_front.1 = f32[1,2048,1,1024]{3,2,1,0:T(1,128)} custom-call(s32[88,128]{1,0:T(8,128)} %slot_table.1.table_ref, f32[3,8,768,128]{3,2,1,0:T(8,128)} %get-tuple-element.11.arrived, f32[16,128,128]{2,1,0:T(8,128)} %get-tuple-element.12.left_raw, f32[8,3,128,128]{3,2,1,0:T(8,128)} %get-tuple-element.13.top_parts, f32[128,128]{1,0:T(8,128)} %get-tuple-element.14.packed, ...), custom_call_target="tpu_custom_call" | custom-call | tf_op jit(solution)/shard_map/update_front/pallas_call | solution.py:610

commit v5 on v4

--- a/solution.py
+++ b/solution.py
@@ -24,8 +24,6 @@
 COL_PICK = 2 * CHILDREN
 ROW_PICK = COL_PICK + COL_SLOTS * CHILDREN
 TABLE_ROWS = ROW_PICK + ROW_SLOTS * CHILDREN
-HALF = PIV // 2
-QUARTER = PIV // 4
 MESH = pl.DeviceIdType.MESH
 ANY = pl.BlockSpec(memory_space=pl.ANY)
 VMEM = pl.BlockSpec(memory_space=pltpu.VMEM)
@@ -111,17 +109,20 @@
 
 def exchange_kernel(table_ref, front_hbm, left_hbm, right_hbm, lead_block, diag, pivots,
                     arrived, left_panel, top_parts, packed, lower, upper,
-                    factors, front, left, contribution, col_chosen, column_0, column_1, column_2,
-                    first_column, raw_lead,
-                    load_sem, ring_send, ring_recv, col_send, col_recv, own_col_sem,
+                    lefts, rights, products, returned, front, contribution, col_chosen, column_0, column_1, column_2,
+                    row_chosen, first_column, raw_lead,
+                    load_sem, ring_send, ring_recv, back_send, back_recv, col_send, col_recv, own_col_sem,
                     top_send, top_recv, row_send, row_recv, own_row_sem, lead_send, lead_recv,
                     spread_send, spread_recv, share_send, share_recv):
     child = lax.axis_index("child")
     group = lax.axis_index("grp")
-    at_y, at_x = group // RING, group % RING
-
-    load_right = pltpu.make_async_copy(right_hbm, factors.at[group], load_sem.at[0])
-    load_left = pltpu.make_async_copy(left_hbm, left, load_sem.at[1])
+    core = lax.rem(child, 2)
+    at_y, at_x = group // RING, lax.rem(group, RING)
+    along = jnp.where(core == 0, at_x, at_y)
+    across = jnp.where(core == 0, at_y, at_x)
+
+    load_right = pltpu.make_async_copy(right_hbm, rights.at[across], load_sem.at[0])
+    load_left = pltpu.make_async_copy(left_hbm, lefts.at[along], load_sem.at[1])
     load_front = pltpu.make_async_copy(front_hbm, front, load_sem.at[2])
     load_right.start()
     load_left.start()
@@ -145,96 +146,111 @@
     lax.fori_loop(1, CHILDREN, greet_child, 0)
     pl.semaphore_wait(barrier, GROUPS + CHILDREN - 2)
 
-    def place(half, first, second):
-        return second * RING + first if half == 0 else first * RING + second
-
     def turn(position, by):
         return lax.rem(position + by + RING, RING)
 
-    def piece(half, block, quarter):
-        if quarter is None:
-            return factors.at[block, pl.ds(half * HALF, HALF)]
-        return factors.at[block, pl.ds(half * HALF + quarter * QUARTER, QUARTER)]
-
-    copies = {}
-
-    def make(key, half, block, quarter, target):
-        number = len(copies)
-        ref = piece(half, block, quarter)
-        copies[key] = pltpu.make_async_remote_copy(
+    def place(u, v):
+        return jnp.where(core == 0, v * RING + u, u * RING + v)
+
+    gathers = {}
+
+    def make(key, blocks, block, chunk, target):
+        number = len(gathers)
+        size = blocks.shape[1] // 2
+        ref = blocks.at[block, pl.ds(chunk * size, size)]
+        gathers[key] = pltpu.make_async_remote_copy(
             src_ref=ref, dst_ref=ref, send_sem=ring_send.at[number], recv_sem=ring_recv.at[number],
             device_id=(child, target), device_id_type=MESH,
         )
 
-    lines = (0, -1, 1, 2)
-    for half in (0, 1):
-        first, second = (at_x, at_y) if half == 0 else (at_y, at_x)
+    for name, blocks, at in (("l", lefts, along), ("r", rights, across)):
         for way in (1, -1):
-            target = place(half, turn(first, way), second)
-            make((half, "a", way), half, place(half, first, second), None, target)
-            make((half, "af", way), half, place(half, turn(first, -way), second),
-                 0 if way == 1 else 1, target)
-        for line in lines:
-            column = turn(first, line)
-            for way in (1, -1):
-                target = place(half, first, turn(second, way))
-                make((half, line, way), half, place(half, column, second), None, target)
-                make((half, line, "f", way), half, place(half, column, turn(second, -way)),
-                     0 if way == 1 else 1, target)
-
-    def start(*key):
-        for half in (0, 1):
-            for way in (1, -1):
-                copies[(half,) + key + (way,)].start()
-
-    def arrive(*key):
-        for half in (0, 1):
-            for way in (1, -1):
-                copies[(half,) + key + (way,)].wait_recv()
-
-    def multiply(offsets):
+            target = place(turn(along, way), across) if name == "l" else place(along, turn(across, way))
+            first = 0 if way == 1 else 1
+            make((name, way, 0), blocks, at, first, target)
+            make((name, way, 1), blocks, at, 1 - first, target)
+            make((name, way, 2), blocks, turn(at, -way), first, target)
+
+    def start(name, step):
+        gathers[(name, 1, step)].start()
+        gathers[(name, -1, step)].start()
+
+    def arrive(name, step):
+        gathers[(name, 1, step)].wait_recv()
+        gathers[(name, -1, step)].wait_recv()
+
+    def return_copy(to, piece):
+        target = turn(along, to)
+        number = to * RING + piece
+        return pltpu.make_async_remote_copy(
+            src_ref=products.at[target, piece], dst_ref=returned.at[along, piece],
+            send_sem=back_send.at[number], recv_sem=back_recv.at[number],
+            device_id=(child, place(target, across)), device_id_type=MESH,
+        )
+
+    def multiply(pairs):
         def one(i, carry):
-            block = jnp.int32(0)
-            for number, (dy, dx) in enumerate(offsets):
-                block = jnp.where(i == number, turn(at_y, dy) * RING + turn(at_x, dx), block)
-            product = full_dot(left[...], factors[block])
-            base = pl.multiple_of(block * ROWS, ROWS)
-            result = front[:, pl.ds(base, ROWS)] - product
-            contribution[2 * block] = result[:, :NB]
-            contribution[2 * block + 1] = result[:, NB:]
-            return carry
-
-        lax.fori_loop(0, len(offsets), one, 0)
-
+            to, line = jnp.int32(0), jnp.int32(0)
+            for number, (pair_to, pair_line) in enumerate(pairs):
+                to = jnp.where(i == number, pair_to, to)
+                line = jnp.where(i == number, pair_line, line)
+            target, piece = turn(along, to), turn(across, line)
+            product = full_dot(lefts[target], rights[piece])
+
+            @pl.when(to == 0)
+            def _():
+                returned[along, piece] = product
+
+            @pl.when(to != 0)
+            def _():
+                products[target, piece] = product
+                return_copy(to, piece).start()
+
+            return carry
+
+        lax.fori_loop(0, len(pairs), one, 0)
+
+    load_left.wait()
+    start("l", 0)
     load_right.wait()
-    start("a")
-    start(0)
-    load_left.wait()
+    start("r", 0)
+    start("l", 1)
+    start("r", 1)
+    multiply([(0, 0)])
+    arrive("l", 0)
+    start("l", 2)
+    arrive("r", 0)
+    start("r", 2)
+    arrive("l", 1)
+    multiply([(1, 0), (3, 0)])
+    arrive("r", 1)
+    multiply([(1, 1), (3, 1), (1, 3), (3, 3), (0, 1), (0, 3)])
+    arrive("l", 2)
+    multiply([(2, 0), (2, 1), (2, 3)])
+    arrive("r", 2)
+    multiply([(2, 2), (1, 2), (3, 2), (0, 2)])
     load_front.wait()
-    multiply([(0, 0)])
-    arrive("a")
-    start("af")
-    start(-1)
-    start(1)
-    arrive(0)
-    start(0, "f")
-    multiply([(0, 1), (0, -1), (1, 0), (-1, 0)])
-    arrive("af")
-    start(2)
-    arrive(0, "f")
-    multiply([(0, 2), (2, 0)])
-    arrive(-1)
-    start(-1, "f")
-    arrive(1)
-    start(1, "f")
-    multiply([(1, 1), (1, -1), (-1, 1), (-1, -1)])
-    arrive(2)
-    start(2, "f")
-    arrive(-1, "f")
-    arrive(1, "f")
-    multiply([(1, 2), (-1, 2), (2, 1), (2, -1)])
-    arrive(2, "f")
-    multiply([(2, 2)])
+
+    def subtract(source, piece):
+        block = place(source, piece)
+        base = pl.multiple_of(block * ROWS, ROWS)
+        result = front[:, pl.ds(base, ROWS)] - returned[source, piece]
+        contribution[2 * block] = result[:, :NB]
+        contribution[2 * block + 1] = result[:, NB:]
+
+    def subtract_own(piece, carry):
+        subtract(along, piece)
+        return carry
+
+    lax.fori_loop(0, RING, subtract_own, 0)
+
+    def subtract_returned(number, carry):
+        to, line = 1 + number // RING, turn(across, lax.rem(number, RING))
+        return_copy(to, line).wait_recv()
+        subtract(turn(along, -to), line)
+        return carry
+
+    lax.fori_loop(0, (RING - 1) * RING, subtract_returned, 0)
 
     by_column = (column_0, column_1, column_2)
 
@@ -274,8 +290,14 @@
     pass_columns(1)
     pass_columns(2)
 
-    for key in copies:
-        copies[key].wait_send()
+    for key in gathers:
+        gathers[key].wait_send()
+
+    def sent_back(number, carry):
+        return_copy(1 + number // RING, lax.rem(number, RING)).wait_send()
+        return carry
+
+    lax.fori_loop(0, (RING - 1) * RING, sent_back, 0)
 
     def top_copy(slot, i):
         return pltpu.make_async_remote_copy(
@@ -284,30 +306,23 @@
             device_id=(lax.rem(child + i, CHILDREN), group), device_id_type=MESH,
         )
 
-    def row_buffer(slot, target):
-        number = slot * CHILDREN + target
-        lanes = pl.multiple_of(lax.rem(number, 2) * NB, NB)
-        return factors.at[number // 2, pl.ds(0, ROW_SLOTS * NB), pl.ds(lanes, NB)]
-
     def row_copy(slot, i):
         target = lax.rem(child + i, CHILDREN)
         return pltpu.make_async_remote_copy(
-            src_ref=row_buffer(slot, target), dst_ref=arrived.at[slot, child],
+            src_ref=row_chosen.at[slot, target], dst_ref=arrived.at[slot, child],
             send_sem=row_send.at[slot * CHILDREN + i], recv_sem=row_recv.at[slot * CHILDREN + i],
             device_id=(target, group), device_id_type=MESH,
         )
 
     def own_row_copy(slot):
         return pltpu.make_async_copy(
-            row_buffer(slot, child), arrived.at[slot, child], own_row_sem.at[slot]
+            row_chosen.at[slot, child], arrived.at[slot, child], own_row_sem.at[slot]
         )
 
     def select_rows(slot, target):
-        number = slot * CHILDREN + target
-        lanes = pl.multiple_of(lax.rem(number, 2) * NB, NB)
         for r in range(ROW_SLOTS):
             tile = by_column[slot][table_ref[ROW_PICK + r * CHILDREN + child, target]]
-            factors[number // 2, pl.ds(r * NB, NB), pl.ds(lanes, NB)] = tile
+            row_chosen[slot, target, pl.ds(r * NB, NB)] = tile
 
     def pass_rows(slot):
         def finish(i, carry):
@@ -499,24 +514,27 @@
         in_specs=[SMEM, ANY, ANY, ANY, VMEM, VMEM, VMEM],
         out_specs=(ANY, VMEM, VMEM, VMEM, VMEM, VMEM),
         scratch_shapes=[
-            pltpu.VMEM((GROUPS, PIV, ROWS), jnp.float32),
+            pltpu.VMEM((RING, ROWS, PIV), jnp.float32),
+            pltpu.VMEM((RING, PIV, ROWS), jnp.float32),
+            pltpu.VMEM((RING, RING, ROWS, ROWS), jnp.float32),
+            pltpu.VMEM((RING, RING, ROWS, ROWS), jnp.float32),
             pltpu.VMEM((ROWS, CB), jnp.float32),
-            pltpu.VMEM((ROWS, PIV), jnp.float32),
             pltpu.VMEM((CBT, ROWS, NB), jnp.float32),
             pltpu.VMEM((COL_SLOTS, GROUPS, 2, NB, NB), jnp.float32),
             pltpu.VMEM((CBT, NB, NB), jnp.float32),
             pltpu.VMEM((CBT, NB, NB), jnp.float32),
             pltpu.VMEM((CBT, NB, NB), jnp.float32),
+            pltpu.VMEM((COL_SLOTS, CHILDREN, ROW_SLOTS * NB, NB), jnp.float32),
             pltpu.VMEM((CHILDREN, ROW_SLOTS, NB, NB), jnp.float32),
             pltpu.VMEM((NB, NB), jnp.float32),
-            dma((ROW_SLOTS,)), dma((40,)), dma((40,)),
+            dma((ROW_SLOTS,)), dma((12,)), dma((12,)), dma((16,)), dma((16,)),
             dma((COL_SLOTS * GROUPS,)), dma((COL_SLOTS * GROUPS,)), dma((COL_SLOTS,)),
             dma((COL_SLOTS * CHILDREN,)), dma((COL_SLOTS * CHILDREN,)),
             dma((COL_SLOTS * CHILDREN,)), dma((COL_SLOTS * CHILDREN,)), dma((COL_SLOTS,)),
             dma((GROUPS,)), dma((1,)), dma((GROUPS,)), dma((1,)), dma((GROUPS,)), dma((GROUPS,)),
         ],
         compiler_params=pltpu.CompilerParams(
-            collective_id=0, has_side_effects=True, vmem_limit_bytes=56 * 2**20
+            collective_id=0, has_side_effects=True, vmem_limit_bytes=60 * 2**20
         ),
         name="exchange",
     )(table, front, left, right, lead_block, diag, pivots)

time: 299 us -> 261 us (0.87)
  Pallas kernels: 296 us -> 260 us
    pallas_call x1, Pallas kernels: 272 us -> 236 us  [exchange(): pl.pallas_call(exchange_kernel, out_shape=(jax.ShapeDtypeStruct((COL_SLOT...]
where the time goes in v5:
time: 261 us; the launch traced here: 260 us
  Pallas kernels  260 us (100%)
    pallas_call x1, Pallas kernels, exchange(): pl.pallas_call(exchange_kernel, out_shape=(jax.ShapeDtypeStruct((COL_SLOT...  236 us
    pallas_call x1, Pallas kernels, update_front(): pl.pallas_call(update_kernel, grid=(TR,), out_shape=jax.ShapeDtypeStruct(...  22.5 us

profile of v5, /device:TPU:1, one launch (start us, length us, event | category | flops | bytes accessed | tf_op | source)
XLA Modules:
  0.0 260.2 jit_solution(9059631387404990809)
XLA Ops:
  0.0 1.8 slot_table.1.table_ref
  1.8 235.9 %exchange.1 = (f32[3,8,768,128]{3,2,1,0:T(8,128)}, f32[16,128,128]{2,1,0:T(8,128)}, f32[8,3,128,128]{3,2,1,0:T(8,128)}, f32[128,128]{1,0:T(8,128)}, f32[128,128]{1,0:T(8,128)}, /*index=5*/f32[128,128]{1,0:T(8,128)}) custom-call(s32[88,128]{1,0:T(8,128)} %slot_table.1.table_ref, f32[256,4096]{1,0:T(8,128)} %bitcast.5, f32[256,1280]{1,0:T(8,128)} %bitcast.6, ...), custom_call_target="tpu_custom_call" | custom-call | tf_op jit(solution)/shard_map/exchange/pallas_call | solution.py:506
  237.7 22.5 %update_front.1 = f32[1,2048,1,1024]{3,2,1,0:T(1,128)} custom-call(s32[88,128]{1,0:T(8,128)} %slot_table.1.table_ref, f32[3,8,768,128]{3,2,1,0:T(8,128)} %get-tuple-element.11.arrived, f32[16,128,128]{2,1,0:T(8,128)} %get-tuple-element.12.left_raw, f32[8,3,128,128]{3,2,1,0:T(8,128)} %get-tuple-element.13.top_parts, f32[128,128]{1,0:T(8,128)} %get-tuple-element.14.packed, ...), custom_call_target="tpu_custom_call" | custom-call | tf_op jit(solution)/shard_map/update_front/pallas_call | solution.py:628

commit v6 on v5

--- a/solution.py
+++ b/solution.py
@@ -18,6 +18,10 @@
 TC = PT // GROUPS
 COL_SLOTS = 3
 ROW_SLOTS = 6
+PARTS = 2
+PART = NB // PARTS
+CHUNKS = COL_SLOTS * PARTS
+STEP = 4
 ROWS = CB // GROUPS
 COL_SLOT = 0
 ROW_SLOT = CHILDREN
@@ -108,12 +112,17 @@
 
 
 def exchange_kernel(table_ref, front_hbm, left_hbm, right_hbm, lead_block, diag, pivots,
-                    arrived, left_panel, top_parts, packed, lower, upper,
-                    lefts, rights, products, returned, front, contribution, col_chosen, column_0, column_1, column_2,
-                    row_chosen, first_column, raw_lead,
+                    arrived, left_panel, right_panel, packed, lower, upper,
+                    lefts, rights, products, returned, front, contribution, col_chosen,
+                    column_0, column_1, column_2, column_3, column_4, column_5,
+                    row_chosen, first_column, raw_lead, lead_parts,
+                    top_own, top_peer, top_sum, top_got,
                     load_sem, ring_send, ring_recv, back_send, back_recv, col_send, col_recv, own_col_sem,
-                    top_send, top_recv, row_send, row_recv, own_row_sem, lead_send, lead_recv,
-                    spread_send, spread_recv, share_send, share_recv):
+                    row_send, row_recv, own_row_sem,
+                    lead_part_send, lead_part_recv, lead_cast_send, lead_cast_recv, lead_send, lead_recv,
+                    spread_send, spread_recv, share_send, share_recv,
+                    peer_send, peer_recv, reduce_send, reduce_recv, top_send, top_recv):
+    by_column = (column_0, column_1, column_2, column_3, column_4, column_5)
     child = lax.axis_index("child")
     group = lax.axis_index("grp")
     core = lax.rem(child, 2)
@@ -235,8 +244,8 @@
         block = place(source, piece)
         base = pl.multiple_of(block * ROWS, ROWS)
         result = front[:, pl.ds(base, ROWS)] - returned[source, piece]
-        contribution[2 * block] = result[:, :NB]
-        contribution[2 * block + 1] = result[:, NB:]
+        contribution[2 * block] = result[:, :NB].reshape(2, PARTS, PART, NB)
+        contribution[2 * block + 1] = result[:, NB:].reshape(2, PARTS, PART, NB)
 
     def subtract_own(piece, carry):
         subtract(along, piece)
@@ -252,43 +261,39 @@
 
     lax.fori_loop(0, (RING - 1) * RING, subtract_returned, 0)
 
-    by_column = (column_0, column_1, column_2)
-
-    def column_target(i):
-        return lax.rem(group + i, GROUPS)
-
-    def column_copy(slot, i):
-        target = column_target(i)
-        return pltpu.make_async_remote_copy(
-            src_ref=col_chosen.at[slot, target],
-            dst_ref=by_column[slot].at[pl.ds(2 * group, 2)],
-            send_sem=col_send.at[slot * GROUPS + i], recv_sem=col_recv.at[slot * GROUPS + i],
+    def column_copy(chunk, i):
+        target = lax.rem(group + i, GROUPS)
+        return pltpu.make_async_remote_copy(
+            src_ref=col_chosen.at[chunk, target],
+            dst_ref=by_column[chunk].at[pl.ds(2 * group, 2)],
+            send_sem=col_send.at[chunk * GROUPS + i], recv_sem=col_recv.at[chunk * GROUPS + i],
             device_id=(child, target), device_id_type=MESH,
         )
 
-    def own_column_copy(slot):
+    def own_column_copy(chunk):
         return pltpu.make_async_copy(
-            col_chosen.at[slot, group], by_column[slot].at[pl.ds(2 * group, 2)],
-            own_col_sem.at[slot],
-        )
-
-    def select_column(slot, target):
-        tile = contribution[table_ref[COL_PICK + slot * CHILDREN + child, target]]
-        col_chosen[slot, target] = tile.reshape(2, NB, NB)
-
-    def pass_columns(slot):
+            col_chosen.at[chunk, group], by_column[chunk].at[pl.ds(2 * group, 2)],
+            own_col_sem.at[chunk],
+        )
+
+    def select_column(chunk, target):
+        slot, part = chunk // PARTS, chunk % PARTS
+        picked = table_ref[COL_PICK + slot * CHILDREN + child, target]
+        for row in range(2):
+            col_chosen[chunk, target, row] = contribution[picked, row, part]
+
+    def pass_columns(chunk):
         def send_column(i, carry):
-            select_column(slot, column_target(i))
-            column_copy(slot, i).start()
+            select_column(chunk, lax.rem(group + i, GROUPS))
+            column_copy(chunk, i).start()
             return carry
 
         lax.fori_loop(1, GROUPS, send_column, 0)
-        select_column(slot, group)
-        own_column_copy(slot).start()
-
-    pass_columns(0)
-    pass_columns(1)
-    pass_columns(2)
+        select_column(chunk, group)
+        own_column_copy(chunk).start()
+
+    for chunk in range(CHUNKS):
+        pass_columns(chunk)
 
     for key in gathers:
         gathers[key].wait_send()
@@ -299,69 +304,67 @@
 
     lax.fori_loop(0, (RING - 1) * RING, sent_back, 0)
 
-    def top_copy(slot, i):
-        return pltpu.make_async_remote_copy(
-            src_ref=top_parts.at[child, slot], dst_ref=top_parts.at[child, slot],
-            send_sem=top_send.at[slot * CHILDREN + i], recv_sem=top_recv.at[slot * CHILDREN + i],
-            device_id=(lax.rem(child + i, CHILDREN), group), device_id_type=MESH,
-        )
-
-    def row_copy(slot, i):
+    def row_copy(chunk, i):
         target = lax.rem(child + i, CHILDREN)
         return pltpu.make_async_remote_copy(
-            src_ref=row_chosen.at[slot, target], dst_ref=arrived.at[slot, child],
-            send_sem=row_send.at[slot * CHILDREN + i], recv_sem=row_recv.at[slot * CHILDREN + i],
+            src_ref=row_chosen.at[chunk, target], dst_ref=arrived.at[chunk, child],
+            send_sem=row_send.at[chunk * CHILDREN + i], recv_sem=row_recv.at[chunk * CHILDREN + i],
             device_id=(target, group), device_id_type=MESH,
         )
 
-    def own_row_copy(slot):
+    def own_row_copy(chunk):
         return pltpu.make_async_copy(
-            row_chosen.at[slot, child], arrived.at[slot, child], own_row_sem.at[slot]
-        )
-
-    def select_rows(slot, target):
+            row_chosen.at[chunk, child], arrived.at[chunk, child], own_row_sem.at[chunk]
+        )
+
+    def select_rows(chunk, target):
         for r in range(ROW_SLOTS):
-            tile = by_column[slot][table_ref[ROW_PICK + r * CHILDREN + child, target]]
-            row_chosen[slot, target, pl.ds(r * NB, NB)] = tile
-
-    def pass_rows(slot):
+            tile = by_column[chunk][table_ref[ROW_PICK + r * CHILDREN + child, target]]
+            row_chosen[chunk, target, pl.ds(r * PART, PART)] = tile
+
+    def pass_rows(chunk):
         def finish(i, carry):
-            column_copy(slot, i).wait_recv()
+            column_copy(chunk, i).wait_recv()
             return carry
 
         lax.fori_loop(1, GROUPS, finish, 0)
-        own_column_copy(slot).wait()
-        top_parts[child, slot] = by_column[slot][table_ref[ROW_PICK + child, 0]]
-
-        def send_top(i, carry):
-            top_copy(slot, i).start()
-            return carry
-
-        lax.fori_loop(1, CHILDREN, send_top, 0)
+        own_column_copy(chunk).wait()
 
         def send_rows(i, carry):
-            select_rows(slot, lax.rem(child + i, CHILDREN))
-            row_copy(slot, i).start()
+            select_rows(chunk, lax.rem(child + i, CHILDREN))
+            row_copy(chunk, i).start()
             return carry
 
         lax.fori_loop(1, CHILDREN, send_rows, 0)
-        select_rows(slot, child)
-        own_row_copy(slot).start()
-
-    def finish_top(slot):
-        def arrive_top(i, carry):
-            top_copy(slot, i).wait_recv()
-            return carry
-
-        lax.fori_loop(1, CHILDREN, arrive_top, 0)
-
-    def finish_rows(slot):
+        select_rows(chunk, child)
+        own_row_copy(chunk).start()
+
+    def finish_rows(chunk):
         def finish(i, carry):
-            row_copy(slot, i).wait_recv()
+            row_copy(chunk, i).wait_recv()
             return carry
 
         lax.fori_loop(1, CHILDREN, finish, 0)
-        own_row_copy(slot).wait()
+        own_row_copy(chunk).wait()
+
+    def top_tile(chunk):
+        return by_column[chunk][table_ref[ROW_PICK + child, 0]]
+
+    lead_here = table_ref[COL_SLOT + child, 0] >= 0
+
+    def lead_part_copy(source):
+        return pltpu.make_async_remote_copy(
+            src_ref=lead_parts.at[source], dst_ref=lead_parts.at[source],
+            send_sem=lead_part_send.at[0], recv_sem=lead_part_recv.at[source],
+            device_id=(0, group), device_id_type=MESH,
+        )
+
+    def lead_cast_copy(target):
+        return pltpu.make_async_remote_copy(
+            src_ref=raw_lead, dst_ref=raw_lead,
+            send_sem=lead_cast_send.at[target], recv_sem=lead_cast_recv.at[0],
+            device_id=(target, group), device_id_type=MESH,
+        )
 
     def lead_copy(target):
         return pltpu.make_async_remote_copy(
@@ -370,6 +373,45 @@
             device_id=(child, target), device_id_type=MESH,
         )
 
+    def send_lead_part():
+        for part in range(PARTS):
+            tile = jnp.where(lead_here, top_tile(part), 0.0)
+            lead_parts[child, pl.ds(part * PART, PART)] = tile
+
+        @pl.when(child != 0)
+        def _():
+            lead_part_copy(child).start()
+
+    def sum_lead():
+        def arrive_part(k, carry):
+            lead_part_copy(k).wait_recv()
+            return carry
+
+        lax.fori_loop(1, CHILDREN, arrive_part, 0)
+        rows = lax.broadcasted_iota(jnp.int32, (NB, NB), 0)
+        cols = lax.broadcasted_iota(jnp.int32, (NB, NB), 1)
+        total = lead_block[...] + jnp.where(rows == cols, diag[0:1, :], 0.0)
+        for k in range(CHILDREN):
+            total = total + lead_parts[k]
+        raw_lead[...] = permute_rows(pivots, total)
+
+        def cast(k, carry):
+            lead_cast_copy(k).start()
+            return carry
+
+        lax.fori_loop(1, CHILDREN, cast, 0)
+
+    def pass_lead():
+        @pl.when(child != 0)
+        def _():
+            lead_cast_copy(0).wait_recv()
+
+        def send_lead(i, carry):
+            lead_copy(i).start()
+            return carry
+
+        lax.fori_loop(1, GROUPS, send_lead, 0)
+
     def spread_copy(target):
         return pltpu.make_async_remote_copy(
             src_ref=left_panel.at[target], dst_ref=left_panel.at[target],
@@ -391,25 +433,57 @@
             device_id=(child, lax.rem(group + i, GROUPS)), device_id_type=MESH,
         )
 
+    at_z = child // 2
+    partner = child + 1 - 2 * core
+
+    def peer_copy():
+        return pltpu.make_async_remote_copy(
+            src_ref=top_own.at[1 - core], dst_ref=top_peer,
+            send_sem=peer_send.at[0], recv_sem=peer_recv.at[0],
+            device_id=(partner, group), device_id_type=MESH,
+        )
+
+    def reduce_copy(i):
+        target = turn(at_z, i)
+        return pltpu.make_async_remote_copy(
+            src_ref=top_sum.at[target], dst_ref=top_got.at[at_z],
+            send_sem=reduce_send.at[i], recv_sem=reduce_recv.at[i],
+            device_id=(2 * target + core, group), device_id_type=MESH,
+        )
+
+    def top_share_copy(i):
+        target = turn(at_z, i)
+        return pltpu.make_async_remote_copy(
+            src_ref=right_panel.at[core, at_z], dst_ref=right_panel.at[core, at_z],
+            send_sem=top_send.at[i], recv_sem=top_recv.at[i],
+            device_id=(2 * target + core, group), device_id_type=MESH,
+        )
+
+    def peer_share_copy():
+        return pltpu.make_async_remote_copy(
+            src_ref=right_panel.at[core], dst_ref=right_panel.at[core],
+            send_sem=peer_send.at[1], recv_sem=peer_recv.at[1],
+            device_id=(partner, group), device_id_type=MESH,
+        )
+
     pass_rows(0)
-    finish_top(0)
-    rows = lax.broadcasted_iota(jnp.int32, (NB, NB), 0)
-    cols = lax.broadcasted_iota(jnp.int32, (NB, NB), 1)
+    pass_rows(1)
 
     @pl.when(group == 0)
     def _():
-        total = lead_block[...] + jnp.where(rows == cols, diag[0:1, :], 0.0)
-        for k in range(CHILDREN):
-            total = total + jnp.where(table_ref[COL_SLOT + k, 0] >= 0, top_parts[k, 0], 0.0)
-        raw_lead[...] = permute_rows(pivots, total)
-
-        def send_lead(i, carry):
-            lead_copy(i).start()
-            return carry
-
-        lax.fori_loop(1, GROUPS, send_lead, 0)
-
-    pass_rows(1)
+        send_lead_part()
+
+    pass_rows(2)
+
+    @pl.when((group == 0) & (child == 0))
+    def _():
+        sum_lead()
+
+    pass_rows(3)
+
+    @pl.when(group == 0)
+    def _():
+        pass_lead()
 
     @pl.when(group != 0)
     def _():
@@ -417,17 +491,30 @@
 
     packed[...] = raw_lead[...]
     factor_tile(packed, lower, upper)
-    pass_rows(2)
-
-    finish_rows(0)
+    pass_rows(4)
+    pass_rows(5)
+
+    for b in range(TC):
+        held = table_ref[COL_SLOT + child, b * GROUPS + group]
+        for part in range(PARTS):
+            total = jnp.zeros((PART, NB), jnp.float32)
+            for slot in range(COL_SLOTS):
+                tile = top_tile(slot * PARTS + part)
+                total = jnp.where(lead_here & (held == slot), tile, total)
+            top_own[b % 2, b // 2, part * PART:(part + 1) * PART] = total
+    peer_copy().start()
+
+    for part in range(PARTS):
+        finish_rows(part)
 
     @pl.when(group == 0)
     def _():
         loads = [
             pltpu.make_async_copy(
-                arrived.at[0, :, pl.ds(r * NB, NB), :], first_column.at[:, r], load_sem.at[r]
+                arrived.at[part, :, pl.ds(r * PART, PART), :], first_column.at[part, :, r],
+                load_sem.at[part * ROW_SLOTS + r],
             )
-            for r in range(ROW_SLOTS)
+            for part in range(PARTS) for r in range(ROW_SLOTS)
         ]
         for load in loads:
             load.start()
@@ -436,13 +523,14 @@
 
         def assemble(i, carry):
             a = lax.rem(i, TR)
-            total = jnp.zeros((NB, NB), jnp.float32)
-            for k in range(CHILDREN):
-                slot = table_ref[ROW_SLOT + k, a * CHILDREN + child]
-                held = (slot >= 0) & (table_ref[COL_SLOT + k, 0] >= 0)
-                tile = first_column[k, jnp.maximum(slot, 0)]
-                total = total + jnp.where(held, tile, 0.0)
-            left_panel[a] = total
+            for part in range(PARTS):
+                total = jnp.zeros((PART, NB), jnp.float32)
+                for k in range(CHILDREN):
+                    slot = table_ref[ROW_SLOT + k, a * CHILDREN + child]
+                    held = (slot >= 0) & (table_ref[COL_SLOT + k, 0] >= 0)
+                    tile = first_column[part, k, jnp.maximum(slot, 0)]
+                    total = total + jnp.where(held, tile, 0.0)
+                left_panel[a, part * PART:(part + 1) * PART] = total
 
             @pl.when(a > 0)
             def _():
@@ -452,6 +540,11 @@
 
         lax.fori_loop(1, TR + 1, assemble, 0)
 
+    peer_copy().wait_recv()
+    top_sum[...] = top_own[core] + top_peer[...]
+    for i in range(1, RING):
+        reduce_copy(i).start()
+
     @pl.when(group != 0)
     def _():
         own_spread().wait_recv()
@@ -463,8 +556,17 @@
         return carry
 
     lax.fori_loop(1, GROUPS, send_share, 0)
-    finish_top(1)
-    finish_top(2)
+
+    for i in range(1, RING):
+        reduce_copy(i).wait_recv()
+    right_panel[core, at_z] = (
+        top_sum[at_z] + top_got[turn(at_z, 1)] + top_got[turn(at_z, 2)] + top_got[turn(at_z, 3)]
+    )
+    for i in range(1, RING):
+        top_share_copy(i).start()
+    for i in range(1, RING):
+        top_share_copy(i).wait_recv()
+    peer_share_copy().start()
 
     def finish_share(i, carry):
         @pl.when(lax.rem(group + i, GROUPS) != 0)
@@ -483,20 +585,40 @@
         return carry
 
     lax.fori_loop(1, GROUPS, finish_share, 0)
-    finish_rows(1)
-    finish_rows(2)
-
-    for slot in range(COL_SLOTS):
+
+    @pl.when((group == 0) & (child == 0))
+    def _():
+        def sent_cast(k, carry):
+            lead_cast_copy(k).wait_send()
+            return carry
+
+        lax.fori_loop(1, CHILDREN, sent_cast, 0)
+
+    @pl.when((group == 0) & (child != 0))
+    def _():
+        lead_part_copy(child).wait_send()
+
+    peer_copy().wait_send()
+    for i in range(1, RING):
+        reduce_copy(i).wait_send()
+        top_share_copy(i).wait_send()
+
+    for chunk in range(CHUNKS):
         def sent_columns(i, carry):
-            column_copy(slot, i).wait_send()
-            return carry
-
+            column_copy(chunk, i).wait_send()
+            return carry
+
+        lax.fori_loop(1, GROUPS, sent_columns, 0)
+
+    for chunk in range(PARTS, CHUNKS):
+        finish_rows(chunk)
+    peer_share_copy().wait()
+
+    for chunk in range(CHUNKS):
         def sent_rows(i, carry):
-            top_copy(slot, i).wait_send()
-            row_copy(slot, i).wait_send()
-            return carry
-
-        lax.fori_loop(1, GROUPS, sent_columns, 0)
+            row_copy(chunk, i).wait_send()
+            return carry
+
         lax.fori_loop(1, CHILDREN, sent_rows, 0)
 
 
@@ -506,9 +628,9 @@
     return pl.pallas_call(
         exchange_kernel,
         out_shape=(
-            jax.ShapeDtypeStruct((COL_SLOTS, CHILDREN, ROW_SLOTS * NB, NB), jnp.float32),
+            jax.ShapeDtypeStruct((CHUNKS, CHILDREN, ROW_SLOTS * PART, NB), jnp.float32),
             jax.ShapeDtypeStruct((TR, NB, NB), jnp.float32),
-            jax.ShapeDtypeStruct((CHILDREN, COL_SLOTS, NB, NB), jnp.float32),
+            jax.ShapeDtypeStruct((2, RING, NB, NB), jnp.float32),
             tile, tile, tile,
         ),
         in_specs=[SMEM, ANY, ANY, ANY, VMEM, VMEM, VMEM],
@@ -519,19 +641,28 @@
             pltpu.VMEM((RING, RING, ROWS, ROWS), jnp.float32),
             pltpu.VMEM((RING, RING, ROWS, ROWS), jnp.float32),
             pltpu.VMEM((ROWS, CB), jnp.float32),
-            pltpu.VMEM((CBT, ROWS, NB), jnp.float32),
-            pltpu.VMEM((COL_SLOTS, GROUPS, 2, NB, NB), jnp.float32),
-            pltpu.VMEM((CBT, NB, NB), jnp.float32),
-            pltpu.VMEM((CBT, NB, NB), jnp.float32),
-            pltpu.VMEM((CBT, NB, NB), jnp.float32),
-            pltpu.VMEM((COL_SLOTS, CHILDREN, ROW_SLOTS * NB, NB), jnp.float32),
-            pltpu.VMEM((CHILDREN, ROW_SLOTS, NB, NB), jnp.float32),
+            pltpu.VMEM((CBT, 2, PARTS, PART, NB), jnp.float32),
+            pltpu.VMEM((CHUNKS, GROUPS, 2, PART, NB), jnp.float32),
+            pltpu.VMEM((CBT, PART, NB), jnp.float32),
+            pltpu.VMEM((CBT, PART, NB), jnp.float32),
+            pltpu.VMEM((CBT, PART, NB), jnp.float32),
+            pltpu.VMEM((CBT, PART, NB), jnp.float32),
+            pltpu.VMEM((CBT, PART, NB), jnp.float32),
+            pltpu.VMEM((CBT, PART, NB), jnp.float32),
+            pltpu.VMEM((CHUNKS, CHILDREN, ROW_SLOTS * PART, NB), jnp.float32),
+            pltpu.VMEM((PARTS, CHILDREN, ROW_SLOTS, PART, NB), jnp.float32),
             pltpu.VMEM((NB, NB), jnp.float32),
-            dma((ROW_SLOTS,)), dma((12,)), dma((12,)), dma((16,)), dma((16,)),
-            dma((COL_SLOTS * GROUPS,)), dma((COL_SLOTS * GROUPS,)), dma((COL_SLOTS,)),
-            dma((COL_SLOTS * CHILDREN,)), dma((COL_SLOTS * CHILDREN,)),
-            dma((COL_SLOTS * CHILDREN,)), dma((COL_SLOTS * CHILDREN,)), dma((COL_SLOTS,)),
-            dma((GROUPS,)), dma((1,)), dma((GROUPS,)), dma((1,)), dma((GROUPS,)), dma((GROUPS,)),
+            pltpu.VMEM((CHILDREN, NB, NB), jnp.float32),
+            pltpu.VMEM((2, RING, NB, NB), jnp.float32),
+            pltpu.VMEM((RING, NB, NB), jnp.float32),
+            pltpu.VMEM((RING, NB, NB), jnp.float32),
+            pltpu.VMEM((RING, NB, NB), jnp.float32),
+            dma((PARTS * ROW_SLOTS,)), dma((12,)), dma((12,)), dma((16,)), dma((16,)),
+            dma((CHUNKS * GROUPS,)), dma((CHUNKS * GROUPS,)), dma((CHUNKS,)),
+            dma((CHUNKS * CHILDREN,)), dma((CHUNKS * CHILDREN,)), dma((CHUNKS,)),
+            dma((1,)), dma((CHILDREN,)), dma((CHILDREN,)), dma((1,)), dma((GROUPS,)), dma((1,)),
+            dma((GROUPS,)), dma((1,)), dma((GROUPS,)), dma((GROUPS,)),
+            dma((2,)), dma((2,)), dma((RING,)), dma((RING,)), dma((RING,)), dma((RING,)),
         ],
         compiler_params=pltpu.CompilerParams(
             collective_id=0, has_side_effects=True, vmem_limit_bytes=60 * 2**20
@@ -545,26 +676,18 @@
     return high, (values - high.astype(jnp.float32)).astype(jnp.bfloat16)
 
 
-def update_kernel(table_ref, arrived, left_raw, top_parts,
+def update_kernel(table_ref, arrived, left_raw, right_panel,
                   packed, lower, upper, diag, pivots, out_ref, right, right_parts, total):
-    a = pl.program_id(0)
+    step = pl.program_id(0)
     child = lax.axis_index("child")
     group = lax.axis_index("grp")
     rows = lax.broadcasted_iota(jnp.int32, (NB, NB), 0)
     cols = lax.broadcasted_iota(jnp.int32, (NB, NB), 1)
 
-    @pl.when(a == 0)
-    def _():
-        right[...] = jnp.zeros_like(right)
-        for k in range(CHILDREN):
-            for b in range(TC):
-                slot = table_ref[COL_SLOT + k, b * GROUPS + group]
-
-                @pl.when((slot >= 0) & (table_ref[COL_SLOT + k, 0] >= 0))
-                def _():
-                    span = pl.ds(b * NB, NB)
-                    right[:, span] = right[:, span] + top_parts[k, slot]
-
+    @pl.when(step == 0)
+    def _():
+        for b in range(TC):
+            right[:, b * NB:(b + 1) * NB] = right_panel[b % 2, b // 2]
         right[...] = full_dot(lower[...], permute_rows(pivots, right[...]))
 
         @pl.when(group == 0)
@@ -576,85 +699,88 @@
         right_parts[NB:2 * NB] = low
         right_parts[2 * NB:] = high
 
-    top = (a == 0) & (child == 0)
-
-    @pl.when(top)
-    def _():
-        total[...] = right[...]
-
-        @pl.when(group == 0)
-        def _():
-            total[:, :NB] = packed[...]
-
-    @pl.when(jnp.logical_not(top))
-    def _():
-        left = full_dot(left_raw[0], upper[...])
-        high, low = split(left)
-        left_parts = jnp.concatenate([high, high, low], axis=1)
-        total[...] = -jnp.dot(
-            left_parts, right_parts[...], preferred_element_type=jnp.float32
-        )
+    left = full_dot(left_raw[...].reshape(STEP * NB, NB), upper[...])
+    high, low = split(left)
+    left_parts = jnp.concatenate([high, high, low], axis=1)
+    total[...] = -jnp.dot(left_parts, right_parts[...], preferred_element_type=jnp.float32)
+
+    def place(row, carry):
+        a = step * STEP + row
         for k in range(CHILDREN):
             row_slot = table_ref[ROW_SLOT + k, a * CHILDREN + child]
 
             @pl.when(row_slot >= 0)
             def _():
-                base = pl.multiple_of(row_slot * NB, NB)
+                base = pl.multiple_of(row_slot * PART, PART)
                 for b in range(TC):
                     col_slot = table_ref[COL_SLOT + k, b * GROUPS + group]
 
                     @pl.when(col_slot >= 0)
                     def _():
-                        span = pl.ds(b * NB, NB)
-                        total[:, span] = total[:, span] + arrived[col_slot, k, pl.ds(base, NB), :]
+                        across = pl.ds(b * NB, NB)
+                        for part in range(PARTS):
+                            down = pl.ds(pl.multiple_of(row * NB, NB) + part * PART, PART)
+                            tile = arrived[col_slot * PARTS + part, k, pl.ds(base, PART), :]
+                            total[down, across] = total[down, across] + tile
 
         on_diag = (lax.rem(group, CHILDREN) == child) & (lax.rem(a, 2) == group // CHILDREN)
 
         @pl.when(on_diag)
         def _():
-            span = pl.ds(pl.multiple_of((a // 2) * NB, NB), NB)
+            across = pl.ds(pl.multiple_of((a // 2) * NB, NB), NB)
+            down = pl.ds(pl.multiple_of(row * NB, NB), NB)
             entries = diag[pl.ds(a * CHILDREN + child, 1), :]
-            total[:, span] = total[:, span] + jnp.where(rows == cols, entries, 0.0)
+            total[down, across] = total[down, across] + jnp.where(rows == cols, entries, 0.0)
+
+        return carry
+
+    lax.fori_loop(0, STEP, place, 0)
+
+    @pl.when(group == 0)
+    def _():
+        total[:, :NB] = left
+
+    @pl.when((step == 0) & (child == 0))
+    def _():
+        total[:NB, :] = right[...]
 
         @pl.when(group == 0)
         def _():
-            total[:, :NB] = left
+            total[:NB, :NB] = packed[...]
 
     out_ref[0, :, 0, :] = total[...]
 
 
-def update_front(table, arrived, left_raw, top_parts,
-                 packed, lower, upper, diag, pivots):
+def update_front(table, arrived, left_raw, right_panel, packed, lower, upper, diag, pivots):
     return pl.pallas_call(
         update_kernel,
-        grid=(TR,),
+        grid=(TR // STEP,),
         out_shape=jax.ShapeDtypeStruct((1, TR * NB, 1, TC * NB), jnp.float32),
         in_specs=[
             SMEM, VMEM,
-            pl.BlockSpec((1, NB, NB), lambda a: (a, 0, 0)),
+            pl.BlockSpec((STEP, NB, NB), lambda a: (a, 0, 0)),
             VMEM, VMEM, VMEM, VMEM, VMEM, VMEM,
         ],
-        out_specs=pl.BlockSpec((1, NB, 1, TC * NB), lambda a: (0, a, 0, 0)),
+        out_specs=pl.BlockSpec((1, STEP * NB, 1, TC * NB), lambda a: (0, a, 0, 0)),
         scratch_shapes=[
             pltpu.VMEM((NB, TC * NB), jnp.float32),
             pltpu.VMEM((3 * NB, TC * NB), jnp.bfloat16),
-            pltpu.VMEM((NB, TC * NB), jnp.float32),
+            pltpu.VMEM((STEP * NB, TC * NB), jnp.float32),
         ],
         compiler_params=pltpu.CompilerParams(vmem_limit_bytes=60 * 2**20),
         name="update_front",
-    )(table, arrived, left_raw, top_parts,
-      packed, lower, upper, diag, pivots)
+    )(table, arrived, left_raw, right_panel, packed, lower, upper, diag, pivots)
 
 
 def body(front_child, left_factor, right_factor, child_map, parent_diag, lead_block, pivots):
     diag = parent_diag.reshape(PT, NB)
     pivot_row = pivots.reshape(1, NB)
     table = slot_table(child_map)
-    arrived, left_raw, top_parts, packed, lower, upper = exchange(
+    arrived, left_raw, right_panel, packed, lower, upper = exchange(
         table, front_child[0], left_factor[0], right_factor[0], lead_block, diag, pivot_row
     )
     return update_front(
-        table, arrived, left_raw, top_parts, packed, lower, upper, diag, pivot_row
+        table, arrived, left_raw, right_panel, packed, lower, upper, diag, pivot_row
     )
 
 

time: 261 us -> 247 us (0.946)
  the two profiles are of different devices: /device:TPU:1 before, /device:TPU:93 now
where the time goes in v6:
time: 247 us
  Pallas kernels  247 us (100%)
    pallas_call x1, Pallas kernels, exchange(): pl.pallas_call(exchange_kernel, out_shape=(jax.ShapeDtypeStruct((CHUNKS,...  226 us
    pallas_call x1, Pallas kernels, update_front(): pl.pallas_call(update_kernel, grid=(TR // STEP,), out_shape=jax.ShapeDtyp...  18.5 us

profile of v6, /device:TPU:93, one launch (start us, length us, event | category | flops | bytes accessed | tf_op | source)
XLA Modules:
  0.0 246.7 jit_solution(14201161181409203552)
XLA Ops:
  0.0 1.8 slot_table.1.table_ref
  1.8 226.4 %exchange.1 = (f32[6,8,384,128]{3,2,1,0:T(8,128)}, f32[16,128,128]{2,1,0:T(8,128)}, f32[2,4,128,128]{3,2,1,0:T(8,128)}, f32[128,128]{1,0:T(8,128)}, f32[128,128]{1,0:T(8,128)}, /*index=5*/f32[128,128]{1,0:T(8,128)}) custom-call(s32[88,128]{1,0:T(8,128)} %slot_table.1.table_ref, f32[256,4096]{1,0:T(8,128)} %bitcast.5, f32[256,1280]{1,0:T(8,128)} %bitcast.6, ...), custom_call_target="tpu_custom_call" | custom-call | tf_op jit(solution)/shard_map/exchange/pallas_call | solution.py:628
  228.2 18.5 %update_front.1 = f32[1,2048,1,1024]{3,2,1,0:T(1,128)} custom-call(s32[88,128]{1,0:T(8,128)} %slot_table.1.table_ref, f32[6,8,384,128]{3,2,1,0:T(8,128)} %get-tuple-element.11.arrived, f32[16,128,128]{2,1,0:T(8,128)} %get-tuple-element.12.left_raw, f32[2,4,128,128]{3,2,1,0:T(8,128)} %get-tuple-element.13.right_panel, f32[128,128]{1,0:T(8,128)} %get-tuple-element.14.packed, ...), custom_call_target="tpu_custom_call" | custom-call | tf_op jit(solution)/shard_map/update_front/pallas_call | solution.py:755

commit v7 on v6

--- a/solution.py
+++ b/solution.py
@@ -322,7 +322,7 @@
             tile = by_column[chunk][table_ref[ROW_PICK + r * CHILDREN + child, target]]
             row_chosen[chunk, target, pl.ds(r * PART, PART)] = tile
 
-    def pass_rows(chunk):
+    def finish_columns(chunk):
         def finish(i, carry):
             column_copy(chunk, i).wait_recv()
             return carry
@@ -330,14 +330,16 @@
         lax.fori_loop(1, GROUPS, finish, 0)
         own_column_copy(chunk).wait()
 
-        def send_rows(i, carry):
+    def send_rows(chunk, first=1, last=CHILDREN):
+        def send(i, carry):
             select_rows(chunk, lax.rem(child + i, CHILDREN))
             row_copy(chunk, i).start()
             return carry
 
-        lax.fori_loop(1, CHILDREN, send_rows, 0)
-        select_rows(chunk, child)
-        own_row_copy(chunk).start()
+        lax.fori_loop(first, last, send, 0)
+        if last == CHILDREN:
+            select_rows(chunk, child)
+            own_row_copy(chunk).start()
 
     def finish_rows(chunk):
         def finish(i, carry):
@@ -466,43 +468,28 @@
             device_id=(partner, group), device_id_type=MESH,
         )
 
-    pass_rows(0)
-    pass_rows(1)
+    finish_columns(0)
+    send_rows(0)
+    finish_columns(1)
 
     @pl.when(group == 0)
     def _():
         send_lead_part()
 
-    pass_rows(2)
+    send_rows(1)
+    finish_columns(2)
 
     @pl.when((group == 0) & (child == 0))
     def _():
         sum_lead()
 
-    pass_rows(3)
+    send_rows(2)
+    finish_columns(3)
+    send_rows(3)
 
     @pl.when(group == 0)
     def _():
         pass_lead()
-
-    @pl.when(group != 0)
-    def _():
-        lead_copy(0).wait_recv()
-
-    packed[...] = raw_lead[...]
-    factor_tile(packed, lower, upper)
-    pass_rows(4)
-    pass_rows(5)
-
-    for b in range(TC):
-        held = table_ref[COL_SLOT + child, b * GROUPS + group]
-        for part in range(PARTS):
-            total = jnp.zeros((PART, NB), jnp.float32)
-            for slot in range(COL_SLOTS):
-                tile = top_tile(slot * PARTS + part)
-                total = jnp.where(lead_here & (held == slot), tile, total)
-            top_own[b % 2, b // 2, part * PART:(part + 1) * PART] = total
-    peer_copy().start()
 
     for part in range(PARTS):
         finish_rows(part)
@@ -540,10 +527,24 @@
 
         lax.fori_loop(1, TR + 1, assemble, 0)
 
+    finish_columns(4)
+    send_rows(4)
+    finish_columns(5)
+
+    for b in range(TC):
+        held = table_ref[COL_SLOT + child, b * GROUPS + group]
+        for part in range(PARTS):
+            total = jnp.zeros((PART, NB), jnp.float32)
+            for slot in range(COL_SLOTS):
+                tile = top_tile(slot * PARTS + part)
+                total = jnp.where(lead_here & (held == slot), tile, total)
+            top_own[b % 2, b // 2, part * PART:(part + 1) * PART] = total
+    peer_copy().start()
     peer_copy().wait_recv()
     top_sum[...] = top_own[core] + top_peer[...]
     for i in range(1, RING):
         reduce_copy(i).start()
+    send_rows(5, 1, RING)
 
     @pl.when(group != 0)
     def _():
@@ -556,6 +557,13 @@
         return carry
 
     lax.fori_loop(1, GROUPS, send_share, 0)
+
+    @pl.when(group != 0)
+    def _():
+        lead_copy(0).wait_recv()
+
+    packed[...] = raw_lead[...]
+    factor_tile(packed, lower, upper)
 
     for i in range(1, RING):
         reduce_copy(i).wait_recv()
@@ -564,6 +572,7 @@
     )
     for i in range(1, RING):
         top_share_copy(i).start()
+    send_rows(5, RING, CHILDREN)
     for i in range(1, RING):
         top_share_copy(i).wait_recv()
     peer_share_copy().start()

time: 247 us -> 230 us (0.931)
  the two profiles are of different devices: /device:TPU:93 before, /device:TPU:1 now
where the time goes in v7:
time: 230 us
  Pallas kernels  230 us (100%)
    pallas_call x1, Pallas kernels, exchange(): pl.pallas_call(exchange_kernel, out_shape=(jax.ShapeDtypeStruct((CHUNKS,...  210 us
    pallas_call x1, Pallas kernels, update_front(): pl.pallas_call(update_kernel, grid=(TR // STEP,), out_shape=jax.ShapeDtyp...  17.9 us

profile of v7, /device:TPU:1, one launch (start us, length us, event | category | flops | bytes accessed | tf_op | source)
XLA Modules:
  0.0 229.9 jit_solution(13412776234203362705)
XLA Ops:
  0.0 1.8 slot_table.1.table_ref
  1.8 210.1 %exchange.1 = (f32[6,8,384,128]{3,2,1,0:T(8,128)}, f32[16,128,128]{2,1,0:T(8,128)}, f32[2,4,128,128]{3,2,1,0:T(8,128)}, f32[128,128]{1,0:T(8,128)}, f32[128,128]{1,0:T(8,128)}, /*index=5*/f32[128,128]{1,0:T(8,128)}) custom-call(s32[88,128]{1,0:T(8,128)} %slot_table.1.table_ref, f32[256,4096]{1,0:T(8,128)} %bitcast.5, f32[256,1280]{1,0:T(8,128)} %bitcast.6, ...), custom_call_target="tpu_custom_call" | custom-call | tf_op jit(solution)/shard_map/exchange/pallas_call | solution.py:637
  211.9 17.9 %update_front.1 = f32[1,2048,1,1024]{3,2,1,0:T(1,128)} custom-call(s32[88,128]{1,0:T(8,128)} %slot_table.1.table_ref, f32[6,8,384,128]{3,2,1,0:T(8,128)} %get-tuple-element.11.arrived, f32[16,128,128]{2,1,0:T(8,128)} %get-tuple-element.12.left_raw, f32[2,4,128,128]{3,2,1,0:T(8,128)} %get-tuple-element.13.right_panel, f32[128,128]{1,0:T(8,128)} %get-tuple-element.14.packed, ...), custom_call_target="tpu_custom_call" | custom-call | tf_op jit(solution)/shard_map/update_front/pallas_call | solution.py:764

commit v8 on v7

--- a/solution.py
+++ b/solution.py
@@ -18,7 +18,7 @@
 TC = PT // GROUPS
 COL_SLOTS = 3
 ROW_SLOTS = 6
-PARTS = 2
+PARTS = 4
 PART = NB // PARTS
 CHUNKS = COL_SLOTS * PARTS
 STEP = 4
@@ -115,6 +115,7 @@
                     arrived, left_panel, right_panel, packed, lower, upper,
                     lefts, rights, products, returned, front, contribution, col_chosen,
                     column_0, column_1, column_2, column_3, column_4, column_5,
+                    column_6, column_7, column_8, column_9, column_10, column_11,
                     row_chosen, first_column, raw_lead, lead_parts,
                     top_own, top_peer, top_sum, top_got,
                     load_sem, ring_send, ring_recv, back_send, back_recv, col_send, col_recv, own_col_sem,
@@ -122,7 +123,10 @@
                     lead_part_send, lead_part_recv, lead_cast_send, lead_cast_recv, lead_send, lead_recv,
                     spread_send, spread_recv, share_send, share_recv,
                     peer_send, peer_recv, reduce_send, reduce_recv, top_send, top_recv):
-    by_column = (column_0, column_1, column_2, column_3, column_4, column_5)
+    by_column = (
+        column_0, column_1, column_2, column_3, column_4, column_5,
+        column_6, column_7, column_8, column_9, column_10, column_11,
+    )
     child = lax.axis_index("child")
     group = lax.axis_index("grp")
     core = lax.rem(child, 2)
@@ -468,24 +472,28 @@
             device_id=(partner, group), device_id_type=MESH,
         )
 
-    finish_columns(0)
-    send_rows(0)
-    finish_columns(1)
+    def pass_chunks(first, last):
+        for chunk in range(first, last):
+            finish_columns(chunk)
+            send_rows(chunk)
+
+    pass_chunks(0, PARTS - 1)
+    finish_columns(PARTS - 1)
 
     @pl.when(group == 0)
     def _():
         send_lead_part()
 
-    send_rows(1)
-    finish_columns(2)
+    send_rows(PARTS - 1)
+    pass_chunks(PARTS, 3 * PARTS // 2 - 1)
+    finish_columns(3 * PARTS // 2 - 1)
 
     @pl.when((group == 0) & (child == 0))
     def _():
         sum_lead()
 
-    send_rows(2)
-    finish_columns(3)
-    send_rows(3)
+    send_rows(3 * PARTS // 2 - 1)
+    pass_chunks(3 * PARTS // 2, 2 * PARTS)
 
     @pl.when(group == 0)
     def _():
@@ -527,9 +535,8 @@
 
         lax.fori_loop(1, TR + 1, assemble, 0)
 
-    finish_columns(4)
-    send_rows(4)
-    finish_columns(5)
+    pass_chunks(2 * PARTS, CHUNKS - 1)
+    finish_columns(CHUNKS - 1)
 
     for b in range(TC):
         held = table_ref[COL_SLOT + child, b * GROUPS + group]
@@ -544,7 +551,7 @@
     top_sum[...] = top_own[core] + top_peer[...]
     for i in range(1, RING):
         reduce_copy(i).start()
-    send_rows(5, 1, RING)
+    send_rows(CHUNKS - 1, 1, RING)
 
     @pl.when(group != 0)
     def _():
@@ -572,7 +579,7 @@
     )
     for i in range(1, RING):
         top_share_copy(i).start()
-    send_rows(5, RING, CHILDREN)
+    send_rows(CHUNKS - 1, RING, CHILDREN)
     for i in range(1, RING):
         top_share_copy(i).wait_recv()
     peer_share_copy().start()
@@ -658,6 +665,12 @@
             pltpu.VMEM((CBT, PART, NB), jnp.float32),
             pltpu.VMEM((CBT, PART, NB), jnp.float32),
             pltpu.VMEM((CBT, PART, NB), jnp.float32),
+            pltpu.VMEM((CBT, PART, NB), jnp.float32),
+            pltpu.VMEM((CBT, PART, NB), jnp.float32),
+            pltpu.VMEM((CBT, PART, NB), jnp.float32),
+            pltpu.VMEM((CBT, PART, NB), jnp.float32),
+            pltpu.VMEM((CBT, PART, NB), jnp.float32),
+            pltpu.VMEM((CBT, PART, NB), jnp.float32),
             pltpu.VMEM((CHUNKS, CHILDREN, ROW_SLOTS * PART, NB), jnp.float32),
             pltpu.VMEM((PARTS, CHILDREN, ROW_SLOTS, PART, NB), jnp.float32),
             pltpu.VMEM((NB, NB), jnp.float32),
@@ -685,9 +698,21 @@
     return high, (values - high.astype(jnp.float32)).astype(jnp.bfloat16)
 
 
-def update_kernel(table_ref, arrived, left_raw, right_panel,
-                  packed, lower, upper, diag, pivots, out_ref, right, right_parts, total):
+def update_kernel(table_ref, arrived_hbm, left_raw, right_panel,
+                  packed, lower, upper, diag, pivots, out_ref,
+                  right, right_parts, total, arrived, arrive_sem):
     step = pl.program_id(0)
+
+    def load(chunk):
+        return pltpu.make_async_copy(
+            arrived_hbm.at[chunk], arrived.at[chunk], arrive_sem.at[chunk]
+        )
+
+    @pl.when(step == 0)
+    def _():
+        for chunk in range(CHUNKS):
+            load(chunk).start()
+
     child = lax.axis_index("child")
     group = lax.axis_index("grp")
     rows = lax.broadcasted_iota(jnp.int32, (NB, NB), 0)
@@ -712,6 +737,11 @@
     high, low = split(left)
     left_parts = jnp.concatenate([high, high, low], axis=1)
     total[...] = -jnp.dot(left_parts, right_parts[...], preferred_element_type=jnp.float32)
+
+    @pl.when(step == 0)
+    def _():
+        for chunk in range(CHUNKS):
+            load(chunk).wait()
 
     def place(row, carry):
         a = step * STEP + row
@@ -766,7 +796,7 @@
         grid=(TR // STEP,),
         out_shape=jax.ShapeDtypeStruct((1, TR * NB, 1, TC * NB), jnp.float32),
         in_specs=[
-            SMEM, VMEM,
+            SMEM, ANY,
             pl.BlockSpec((STEP, NB, NB), lambda a: (a, 0, 0)),
             VMEM, VMEM, VMEM, VMEM, VMEM, VMEM,
         ],
@@ -775,6 +805,8 @@
             pltpu.VMEM((NB, TC * NB), jnp.float32),
             pltpu.VMEM((3 * NB, TC * NB), jnp.bfloat16),
             pltpu.VMEM((STEP * NB, TC * NB), jnp.float32),
+            pltpu.VMEM((CHUNKS, CHILDREN, ROW_SLOTS * PART, NB), jnp.float32),
+            pltpu.SemaphoreType.DMA((CHUNKS,)),
         ],
         compiler_params=pltpu.CompilerParams(vmem_limit_bytes=60 * 2**20),
         name="update_front",

time: 230 us -> 229 us (level)
  no operation moved by 1% of the time
where the time goes in v8:
time: 229 us
  Pallas kernels  228 us (100%)
    pallas_call x1, Pallas kernels, exchange(): pl.pallas_call(exchange_kernel, out_shape=(jax.ShapeDtypeStruct((CHUNKS,...  209 us
    pallas_call x1, Pallas kernels, update_front(): pl.pallas_call(update_kernel, grid=(TR // STEP,), out_shape=jax.ShapeDtyp...  17.8 us

profile of v8, /device:TPU:1, one launch (start us, length us, event | category | flops | bytes accessed | tf_op | source)
XLA Modules:
  0.0 228.6 jit_solution(3338409339132584499)
XLA Ops:
  0.0 1.8 slot_table.1.table_ref
  1.8 208.8 %exchange.1 = (f32[12,8,192,128]{3,2,1,0:T(8,128)}, f32[16,128,128]{2,1,0:T(8,128)}, f32[2,4,128,128]{3,2,1,0:T(8,128)}, f32[128,128]{1,0:T(8,128)}, f32[128,128]{1,0:T(8,128)}, /*index=5*/f32[128,128]{1,0:T(8,128)}) custom-call(s32[88,128]{1,0:T(8,128)} %slot_table.1.table_ref, f32[256,4096]{1,0:T(8,128)} %bitcast.5, f32[256,1280]{1,0:T(8,128)} %bitcast.6, ...), custom_call_target="tpu_custom_call" | custom-call | tf_op jit(solution)/shard_map/exchange/pallas_call | solution.py:644
  210.6 17.8 %update_front.1 = f32[1,2048,1,1024]{3,2,1,0:T(1,128)} custom-call(s32[88,128]{1,0:T(8,128)} %slot_table.1.table_ref, f32[12,8,192,128]{3,2,1,0:T(8,128)} %get-tuple-element.11.arrived_hbm, f32[16,128,128]{2,1,0:T(8,128)} %get-tuple-element.12.left_raw, f32[2,4,128,128]{3,2,1,0:T(8,128)} %get-tuple-element.13.right_panel, ...), custom_call_target="tpu_custom_call" | custom-call | tf_op jit(solution)/shard_map/update_front/pallas_call | solution.py:794

commit v9 on v8

--- a/solution.py
+++ b/solution.py
@@ -38,6 +38,15 @@
     return jnp.dot(a, b, precision=lax.Precision.HIGHEST, preferred_element_type=jnp.float32)
 
 
+def permute_columns(pivots, values):
+    rows = lax.broadcasted_iota(jnp.int32, (NB, NB), 0)
+    chosen = jnp.where(rows == pivots[...], 1.0, 0.0)
+    return lax.dot_general(
+        values, chosen, (((1,), (1,)), ((), ())),
+        precision=lax.Precision.HIGHEST, preferred_element_type=jnp.float32,
+    )
+
+
 def table_kernel(map_ref, table_ref):
     lanes = lax.broadcasted_iota(jnp.int32, (CHILDREN, PT), 1)
     tiles = map_ref[...]
@@ -572,6 +581,30 @@
     packed[...] = raw_lead[...]
     factor_tile(packed, lower, upper)
 
+    def finish_share(i, carry):
+        @pl.when(lax.rem(group + i, GROUPS) != 0)
+        def _():
+            share_copy(i).wait_send()
+
+        @pl.when(group != 0)
+        def _():
+            share_copy(i).wait_recv()
+
+        @pl.when(group == 0)
+        def _():
+            lead_copy(i).wait_send()
+            spread_copy(i).wait_send()
+
+        return carry
+
+    lax.fori_loop(1, GROUPS, finish_share, 0)
+
+    for quarter in range(TR // STEP):
+        span = slice(quarter * STEP, (quarter + 1) * STEP)
+        raw = left_panel[span].reshape(STEP * NB, NB)
+        left_panel[span] = full_dot(raw, upper[...]).reshape(STEP, NB, NB)
+    lower[...] = permute_columns(pivots, lower[...])
+
     for i in range(1, RING):
         reduce_copy(i).wait_recv()
     right_panel[core, at_z] = (
@@ -583,24 +616,6 @@
     for i in range(1, RING):
         top_share_copy(i).wait_recv()
     peer_share_copy().start()
-
-    def finish_share(i, carry):
-        @pl.when(lax.rem(group + i, GROUPS) != 0)
-        def _():
-            share_copy(i).wait_send()
-
-        @pl.when(group != 0)
-        def _():
-            share_copy(i).wait_recv()
-
-        @pl.when(group == 0)
-        def _():
-            lead_copy(i).wait_send()
-            spread_copy(i).wait_send()
-
-        return carry
-
-    lax.fori_loop(1, GROUPS, finish_share, 0)
 
     @pl.when((group == 0) & (child == 0))
     def _():
@@ -699,7 +714,7 @@
 
 
 def update_kernel(table_ref, arrived_hbm, left_raw, right_panel,
-                  packed, lower, upper, diag, pivots, out_ref,
+                  packed, lower, diag, out_ref,
                   right, right_parts, total, arrived, arrive_sem):
     step = pl.program_id(0)
 
@@ -722,7 +737,7 @@
     def _():
         for b in range(TC):
             right[:, b * NB:(b + 1) * NB] = right_panel[b % 2, b // 2]
-        right[...] = full_dot(lower[...], permute_rows(pivots, right[...]))
+        right[...] = full_dot(lower[...], right[...])
 
         @pl.when(group == 0)
         def _():
@@ -733,7 +748,7 @@
         right_parts[NB:2 * NB] = low
         right_parts[2 * NB:] = high
 
-    left = full_dot(left_raw[...].reshape(STEP * NB, NB), upper[...])
+    left = left_raw[...].reshape(STEP * NB, NB)
     high, low = split(left)
     left_parts = jnp.concatenate([high, high, low], axis=1)
     total[...] = -jnp.dot(left_parts, right_parts[...], preferred_element_type=jnp.float32)
@@ -790,7 +805,7 @@
     out_ref[0, :, 0, :] = total[...]
 
 
-def update_front(table, arrived, left_raw, right_panel, packed, lower, upper, diag, pivots):
+def update_front(table, arrived, left_raw, right_panel, packed, lower, diag):
     return pl.pallas_call(
         update_kernel,
         grid=(TR // STEP,),
@@ -798,7 +813,7 @@
         in_specs=[
             SMEM, ANY,
             pl.BlockSpec((STEP, NB, NB), lambda a: (a, 0, 0)),
-            VMEM, VMEM, VMEM, VMEM, VMEM, VMEM,
+            VMEM, VMEM, VMEM, VMEM,
         ],
         out_specs=pl.BlockSpec((1, STEP * NB, 1, TC * NB), lambda a: (0, a, 0, 0)),
         scratch_shapes=[
@@ -810,19 +825,17 @@
         ],
         compiler_params=pltpu.CompilerParams(vmem_limit_bytes=60 * 2**20),
         name="update_front",
-    )(table, arrived, left_raw, right_panel, packed, lower, upper, diag, pivots)
+    )(table, arrived, left_raw, right_panel, packed, lower, diag)
 
 
 def body(front_child, left_factor, right_factor, child_map, parent_diag, lead_block, pivots):
     diag = parent_diag.reshape(PT, NB)
     pivot_row = pivots.reshape(1, NB)
     table = slot_table(child_map)
-    arrived, left_raw, right_panel, packed, lower, upper = exchange(
+    arrived, left_raw, right_panel, packed, lower, _ = exchange(
         table, front_child[0], left_factor[0], right_factor[0], lead_block, diag, pivot_row
     )
-    return update_front(
-        table, arrived, left_raw, right_panel, packed, lower, upper, diag, pivot_row
-    )
+    return update_front(table, arrived, left_raw, right_panel, packed, lower, diag)
 
 
 def solution(mesh):

time: 229 us -> 227 us (level)
  no operation moved by 1% of the time
where the time goes in v9:
time: 227 us
  Pallas kernels  227 us (100%)
    pallas_call x1, Pallas kernels, exchange(): pl.pallas_call(exchange_kernel, out_shape=(jax.ShapeDtypeStruct((CHUNKS,...  209 us
    pallas_call x1, Pallas kernels, update_front(): pl.pallas_call(update_kernel, grid=(TR // STEP,), out_shape=jax.ShapeDtyp...  16.4 us

profile of v9, /device:TPU:1, one launch (start us, length us, event | category | flops | bytes accessed | tf_op | source)
XLA Modules:
  0.0 227.2 jit_solution(17419832341875528075)
XLA Ops:
  0.0 1.8 slot_table.1.table_ref
  1.8 208.8 %exchange.1 = (f32[12,8,192,128]{3,2,1,0:T(8,128)}, f32[16,128,128]{2,1,0:T(8,128)}, f32[2,4,128,128]{3,2,1,0:T(8,128)}, f32[128,128]{1,0:T(8,128)}, f32[128,128]{1,0:T(8,128)}, /*index=5*/f32[128,128]{1,0:T(8,128)}) custom-call(s32[88,128]{1,0:T(8,128)} %slot_table.1.table_ref, f32[256,4096]{1,0:T(8,128)} %bitcast.5, f32[256,1280]{1,0:T(8,128)} %bitcast.6, ...), custom_call_target="tpu_custom_call" | custom-call | tf_op jit(solution)/shard_map/exchange/pallas_call | solution.py:659
  210.6 16.4 %update_front.1 = f32[1,2048,1,1024]{3,2,1,0:T(1,128)} custom-call(s32[88,128]{1,0:T(8,128)} %slot_table.1.table_ref, f32[12,8,192,128]{3,2,1,0:T(8,128)} %get-tuple-element.10.arrived_hbm, f32[16,128,128]{2,1,0:T(8,128)} %get-tuple-element.11.left_raw, f32[2,4,128,128]{3,2,1,0:T(8,128)} %get-tuple-element.12.right_panel, ...), custom_call_target="tpu_custom_call" | custom-call | tf_op jit(solution)/shard_map/update_front/pallas_call | solution.py:809

commit v10 on v9

--- a/solution.py
+++ b/solution.py
@@ -176,21 +176,24 @@
 
     gathers = {}
 
-    def make(key, blocks, block, chunk, target):
+    def make(key, blocks, block, chunk, target, own=None):
         number = len(gathers)
         size = blocks.shape[1] // 2
         ref = blocks.at[block, pl.ds(chunk * size, size)]
+        source = ref if own is None else own.at[pl.ds(chunk * size, size)]
         gathers[key] = pltpu.make_async_remote_copy(
-            src_ref=ref, dst_ref=ref, send_sem=ring_send.at[number], recv_sem=ring_recv.at[number],
+            src_ref=source, dst_ref=ref, send_sem=ring_send.at[number], recv_sem=ring_recv.at[number],
             device_id=(child, target), device_id_type=MESH,
         )
 
-    for name, blocks, at in (("l", lefts, along), ("r", rights, across)):
+    for name, blocks, at, own in (
+        ("l", lefts, along, left_hbm), ("r", rights, across, right_hbm)
+    ):
         for way in (1, -1):
             target = place(turn(along, way), across) if name == "l" else place(along, turn(across, way))
             first = 0 if way == 1 else 1
-            make((name, way, 0), blocks, at, first, target)
-            make((name, way, 1), blocks, at, 1 - first, target)
+            make((name, way, 0), blocks, at, first, target, own)
+            make((name, way, 1), blocks, at, 1 - first, target, own)
             make((name, way, 2), blocks, turn(at, -way), first, target)
 
     def start(name, step):
@@ -232,12 +235,12 @@
 
         lax.fori_loop(0, len(pairs), one, 0)
 
-    load_left.wait()
     start("l", 0)
-    load_right.wait()
     start("r", 0)
     start("l", 1)
     start("r", 1)
+    load_left.wait()
+    load_right.wait()
     multiply([(0, 0)])
     arrive("l", 0)
     start("l", 2)
@@ -274,8 +277,12 @@
 
     lax.fori_loop(0, (RING - 1) * RING, subtract_returned, 0)
 
+    def column_target(i):
+        by = lax.rem(5 * i, GROUPS)
+        return turn(at_y, by // RING) * RING + turn(at_x, lax.rem(by, RING))
+
     def column_copy(chunk, i):
-        target = lax.rem(group + i, GROUPS)
+        target = column_target(i)
         return pltpu.make_async_remote_copy(
             src_ref=col_chosen.at[chunk, target],
             dst_ref=by_column[chunk].at[pl.ds(2 * group, 2)],
@@ -297,7 +304,7 @@
 
     def pass_columns(chunk):
         def send_column(i, carry):
-            select_column(chunk, lax.rem(group + i, GROUPS))
+            select_column(chunk, column_target(i))
             column_copy(chunk, i).start()
             return carry
 

time: 227 us -> 226 us (level)
  no operation moved by 1% of the time
where the time goes in v10:
time: 226 us
  Pallas kernels  226 us (100%)
    pallas_call x1, Pallas kernels, exchange(): pl.pallas_call(exchange_kernel, out_shape=(jax.ShapeDtypeStruct((CHUNKS,...  208 us
    pallas_call x1, Pallas kernels, update_front(): pl.pallas_call(update_kernel, grid=(TR // STEP,), out_shape=jax.ShapeDtyp...  15.7 us

profile of v10, /device:TPU:1, one launch (start us, length us, event | category | flops | bytes accessed | tf_op | source)
XLA Modules:
  0.0 225.9 jit_solution(7645166081011170968)
XLA Ops:
  0.0 1.8 slot_table.1.table_ref
  1.8 208.2 %exchange.1 = (f32[12,8,192,128]{3,2,1,0:T(8,128)}, f32[16,128,128]{2,1,0:T(8,128)}, f32[2,4,128,128]{3,2,1,0:T(8,128)}, f32[128,128]{1,0:T(8,128)}, f32[128,128]{1,0:T(8,128)}, /*index=5*/f32[128,128]{1,0:T(8,128)}) custom-call(s32[88,128]{1,0:T(8,128)} %slot_table.1.table_ref, f32[256,4096]{1,0:T(8,128)} %bitcast.5, f32[256,1280]{1,0:T(8,128)} %bitcast.6, ...), custom_call_target="tpu_custom_call" | custom-call | tf_op jit(solution)/shard_map/exchange/pallas_call | solution.py:666
  210.0 15.7 %update_front.1 = f32[1,2048,1,1024]{3,2,1,0:T(1,128)} custom-call(s32[88,128]{1,0:T(8,128)} %slot_table.1.table_ref, f32[12,8,192,128]{3,2,1,0:T(8,128)} %get-tuple-element.10.arrived_hbm, f32[16,128,128]{2,1,0:T(8,128)} %get-tuple-element.11.left_raw, f32[2,4,128,128]{3,2,1,0:T(8,128)} %get-tuple-element.12.right_panel, ...), custom_call_target="tpu_custom_call" | custom-call | tf_op jit(solution)/shard_map/update_front/pallas_call | solution.py:816
